TPU v7x, 128 devices: a whole 4x4x4 slice. The times are simulated.
128 devices in a mesh: gx: 16 (over z, x), gy: 8 (over y, core).
Axes of the slice: x: 4, y: 4, z: 4, core: 2. Of those that a mesh axis runs over, the one named last changes fastest.
Arguments:
- offsets: float32 [24576, 3, 128], P(('gx', 'gy')), may hold values from 0 to 1
- velocity: float32 [24576, 3, 128], P(('gx', 'gy')), may hold values from -6 to 6
- strain: float32 [24576, 6, 128], P(('gx', 'gy')), may hold values from -3 to 3
- cells: int32 [24576, 128], P(('gx', 'gy')), may hold values from 0 to 511
- materials: int32 [24576, 128], P(('gx', 'gy')), may hold values from 0 to 3
- counts: int32 [24576], P(('gx', 'gy')), may hold values from 1 to 128, 2359296 in all
- block_dest: int32 [24576, 1], P(('gx', 'gy')), may hold values from 0 to 127; in each aligned block of 192 rows (0 to 191, 192 to 383, ...) at most 2 rows name the same one
- material_params: float32 [3, 4], replicated, may hold values from 0.5 to 2
Outputs:
- new_velocity: float32 [24576, 3, 128], P(('gx', 'gy'))
- new_strain: float32 [24576, 6, 128], P(('gx', 'gy'))
- grid_velocity: float32 [3, 32, 16, 128], P(None, 'gx', 'gy')
Inputs may be any that keep to these rules, and one draw needn't show every extreme that they name: `block_dest`: the 192 blocks of one owner device name one patch at most 2 times, and some owner reaches 2.
All inputs are finite; a program needn't handle non-finite values. No bound on the sum of `counts` on one device may be relied on, other than what follows from the above.
Results may differ from a plain program's by a relative error of at most 0.00015.
Values sent between devices are 32-bit elements; how exact they have to be, the bound alone decides.
A program may use at most 64 MiB of HBM per device.

v0:
```python
import math

import jax
import jax.numpy as jnp
from jax import lax
from jax.sharding import PartitionSpec as P

PXC = 2
PYC = 2
NZ = 128
NMAT = 4


DT_STEP = 0.25
VOLUME = 0.5
GRAVITY = 1.0
MASS_FLOOR = 0.25
HIGH = lax.Precision.HIGHEST


def passed_along(value, axis, steps):
    count = lax.axis_size(axis)
    leading, last = (max(0, -steps), min(count, count - steps))
    return lax.ppermute(value, axis, [(source, source + steps) for source in range(leading, last)])


def corner_terms(fracs, corner):
    weights = []
    signs = []
    for axis_num in range(3):
        if corner[axis_num]:
            weights.append(fracs[axis_num])
            signs.append(1.0)
        else:
            weights.append(1.0 - fracs[axis_num])
            signs.append(-1.0)
    weight = weights[0] * weights[1] * weights[2]
    gradient = (
        signs[0] * weights[1] * weights[2],
        weights[0] * signs[1] * weights[2],
        weights[0] * weights[1] * signs[2],
    )
    return (weight, gradient)


def stress_rows(strains, shear):
    trace_term = shear * (strains[0] + strains[1] + strains[2])
    s_xx = 2.0 * shear * strains[0] + trace_term
    s_yy = 2.0 * shear * strains[1] + trace_term
    s_zz = 2.0 * shear * strains[2] + trace_term
    s_xy = 2.0 * shear * strains[3]
    s_xz = 2.0 * shear * strains[4]
    s_yz = 2.0 * shear * strains[5]
    return ((s_xx, s_xy, s_xz), (s_xy, s_yy, s_yz), (s_xz, s_yz, s_zz))


def return_map(strains, grads, limit):
    trial = [
        strains[0] + DT_STEP * grads[0][0],
        strains[1] + DT_STEP * grads[1][1],
        strains[2] + DT_STEP * grads[2][2],
        strains[3] + DT_STEP * 0.5 * (grads[0][1] + grads[1][0]),
        strains[4] + DT_STEP * 0.5 * (grads[0][2] + grads[2][0]),
        strains[5] + DT_STEP * 0.5 * (grads[1][2] + grads[2][1]),
    ]
    mean_part = (trial[0] + trial[1] + trial[2]) / 3.0
    devs = [
        trial[0] - mean_part,
        trial[1] - mean_part,
        trial[2] - mean_part,
        trial[3],
        trial[4],
        trial[5],
    ]
    magnitude = jnp.sqrt(
        devs[0] * devs[0]
        + devs[1] * devs[1]
        + devs[2] * devs[2]
        + 2.0 * (devs[3] * devs[3] + devs[4] * devs[4] + devs[5] * devs[5])
    )
    factor = limit / jnp.maximum(magnitude, limit)
    return [
        mean_part + factor * devs[0],
        mean_part + factor * devs[1],
        mean_part + factor * devs[2],
        factor * devs[3],
        factor * devs[4],
        factor * devs[5],
    ]


def particle_view(fpart, ipart, material_params):
    cell_raw = ipart[0]
    is_live = cell_raw >= 0
    live_float = is_live.astype(jnp.float32)
    cell_safe = jnp.maximum(cell_raw, 0)
    cell_z = cell_safe % NZ
    cell_y = cell_safe // NZ % PYC
    cell_x = cell_safe // (NZ * PYC)
    plane = cell_x * (PYC + 1) + cell_y
    onehot = (ipart[1][None] == jnp.arange(NMAT, dtype=jnp.int32)[:, None]).astype(jnp.float32)
    props = jnp.dot(material_params, onehot, precision=HIGH)
    fracs = (fpart[0], fpart[1], fpart[2])
    speeds = [fpart[3], fpart[4], fpart[5]]
    strains = [fpart[6 + comp] for comp in range(6)]
    return (live_float, plane, cell_z, props, fracs, speeds, strains)


def patch_step(got_float, got_int, material_params):
    slots = got_float.shape[0]
    width = got_float.shape[2]
    group = math.gcd(slots, max(1, 2048 // width))
    nblk = slots // group
    rows_blk = group * width
    planes = (PXC + 1) * (PYC + 1)

    def to_rows(arr):
        kinds = arr.shape[1]
        return (
            arr.reshape(nblk, group, kinds, width)
            .transpose(0, 2, 1, 3)
            .reshape(nblk, kinds, rows_blk)
        )

    float_rows = to_rows(got_float)
    int_rows = to_rows(got_int)
    plane_iota = jnp.arange(planes, dtype=jnp.int32)[:, None]
    depth_iota = jnp.arange(NZ, dtype=jnp.int32)[:, None]

    def scatter_step(grid, parts):
        fpart, ipart = parts
        live_float, plane, cell_z, props, fracs, speeds, strains = particle_view(
            fpart, ipart, material_params
        )
        masses, shear = (props[0], props[1])
        stress = stress_rows(strains, shear)
        for lift in range(2):
            gathered = jnp.zeros((4, planes, rows_blk), jnp.float32)
            for step_x in range(2):
                for step_y in range(2):
                    weight, gradient = corner_terms(fracs, (step_x, step_y, lift))
                    rows = [weight * masses]
                    for comp in range(3):
                        force = (
                            stress[comp][0] * gradient[0]
                            + stress[comp][1] * gradient[1]
                            + stress[comp][2] * gradient[2]
                        )
                        rows.append(weight * masses * speeds[comp] - DT_STEP * VOLUME * force)
                    contrib = jnp.stack(rows) * live_float[None]
                    select = (plane_iota == (plane + step_x * (PYC + 1) + step_y)[None]).astype(
                        jnp.float32
                    )
                    gathered = gathered + select[None] * contrib[:, None]
            zone = (depth_iota == (cell_z + lift)[None]).astype(jnp.float32)
            grid = grid + jnp.einsum("qxp,zp->qxz", gathered, zone, precision=HIGH)
        return (grid, None)

    grid, unused = lax.scan(
        scatter_step, jnp.zeros((4, planes, NZ), jnp.float32), (float_rows, int_rows)
    )
    grid = grid.reshape(4, PXC + 1, PYC + 1, NZ)
    from_left = passed_along(grid[:, PXC], "gx", 1)
    grid = grid[:, :PXC].at[:, 0].add(from_left)
    from_below = passed_along(grid[:, :, PYC], "gy", 1)
    grid = grid[:, :, :PYC].at[:, :, 0].add(from_below)
    node_mass = grid[0]
    momentum = grid[1:4]
    momentum = momentum.at[2].add(-DT_STEP * GRAVITY * node_mass)
    node_vel = momentum / jnp.maximum(node_mass, MASS_FLOOR)[None]
    above = (jnp.arange(NZ, dtype=jnp.int32) > 0).astype(jnp.float32)
    node_vel = node_vel * above[None, None, None, :]
    upper_y = passed_along(node_vel[:, :, 0], "gy", -1)
    ext_y = jnp.concatenate([node_vel, upper_y[:, :, None]], axis=2)
    upper_x = passed_along(ext_y[:, 0], "gx", -1)
    ext_vel = jnp.concatenate([ext_y, upper_x[:, None]], axis=1).reshape(3, planes, NZ)

    def gather_step(carry, parts):
        fpart, ipart = parts
        live_float, plane, cell_z, props, fracs, speeds, strains = particle_view(
            fpart, ipart, material_params
        )
        limit = props[2]
        new_speed = [jnp.zeros_like(fracs[0]) for comp in range(3)]
        grads = [[jnp.zeros_like(fracs[0]) for col in range(3)] for row in range(3)]
        for lift in range(2):
            zone = (depth_iota == (cell_z + lift)[None]).astype(jnp.float32)
            columns = jnp.einsum("kxz,zp->kxp", ext_vel, zone, precision=HIGH)
            for step_x in range(2):
                for step_y in range(2):
                    weight, gradient = corner_terms(fracs, (step_x, step_y, lift))
                    select = (plane_iota == (plane + step_x * (PYC + 1) + step_y)[None]).astype(
                        jnp.float32
                    )
                    picked = jnp.sum(select[None] * columns, axis=1) * live_float[None]
                    for comp in range(3):
                        new_speed[comp] = new_speed[comp] + weight * picked[comp]
                        for col in range(3):
                            grads[comp][col] = grads[comp][col] + picked[comp] * gradient[col]
        new_strains = return_map(strains, grads, limit)
        results = jnp.stack(new_speed + new_strains, axis=0) * live_float[None]
        return (carry, results)

    unused, results = lax.scan(gather_step, jnp.zeros((), jnp.float32), (float_rows, int_rows))
    results = results.reshape(nblk, 9, group, width).transpose(0, 2, 1, 3).reshape(slots, 9, width)
    return (results, node_vel)


def shards(offsets, velocity, strain, cells, materials, counts, block_dest, material_params):
    blocks = cells.shape[0]
    width = cells.shape[1]
    size_x = lax.axis_size("gx")
    size_y = lax.axis_size("gy")
    devices = size_x * size_y
    capacity = max(2, (5 * blocks + 4 * devices - 1) // (4 * devices))
    slots = devices * capacity
    dest = block_dest[:, 0]
    order = jnp.arange(blocks, dtype=jnp.int32)
    earlier = order[:, None] > order[None, :]
    same_dest = dest[:, None] == dest[None, :]
    rank = jnp.sum((earlier & same_dest).astype(jnp.int32), axis=1)
    slot = dest * capacity + rank
    placing = (slot[:, None] == jnp.arange(slots, dtype=jnp.int32)[None, :]).astype(jnp.float32)
    is_live = jnp.arange(width, dtype=jnp.int32)[None, :] < counts[:, None]
    cell_code = jnp.where(is_live, cells + 1, 0)
    payload = jnp.concatenate([offsets, velocity, strain], axis=1)
    labels = jnp.stack([cell_code, materials], axis=1).astype(jnp.float32)
    send_float = jnp.einsum("bs,bkw->skw", placing, payload, precision=HIGH)
    label_slots = jnp.einsum("bs,bkw->skw", placing, labels, precision=HIGH)
    send_int = jnp.floor(label_slots + 0.5).astype(jnp.int32)
    send_int = jnp.concatenate([send_int[:, :1] - 1, send_int[:, 1:]], axis=1)
    got_float, got_int = (
        lax.all_to_all(
            send_float.reshape(devices, capacity, 12, width),
            ("gx", "gy"),
            split_axis=0,
            concat_axis=0,
            tiled=True,
        ),
        lax.all_to_all(
            send_int.reshape(devices, capacity, 2, width),
            ("gx", "gy"),
            split_axis=0,
            concat_axis=0,
            tiled=True,
        ),
    )
    got_float = got_float.reshape(slots, 12, width)
    got_int = got_int.reshape(slots, 2, width)
    results, node_vel = patch_step(got_float, got_int, material_params)
    returned = lax.all_to_all(
        results.reshape(devices, capacity, 9, width),
        ("gx", "gy"),
        split_axis=0,
        concat_axis=0,
        tiled=True,
    )
    returned = returned.reshape(slots, 9, width)
    picked = jnp.einsum("bs,skw->bkw", placing, returned, precision=HIGH)
    return (picked[:, :3], picked[:, 3:], node_vel)


def solution(mesh):
    in_specs = (
        P(("gx", "gy"), None, None),
        P(("gx", "gy"), None, None),
        P(("gx", "gy"), None, None),
        P(("gx", "gy"), None),
        P(("gx", "gy"), None),
        P(("gx", "gy")),
        P(("gx", "gy"), None),
        P(),
    )
    out_specs = (
        P(("gx", "gy"), None, None),
        P(("gx", "gy"), None, None),
        P(None, "gx", "gy", None),
    )
    return jax.shard_map(shards, mesh=mesh, in_specs=in_specs, out_specs=out_specs, check_vma=False)
```

profile of v0, /device:TPU:1, one launch (start us, length us, event | category | flops | bytes accessed | tf_op | source)
XLA Modules:
  0.0 228.8 jit_solution(2636857905669805596)
XLA Ops:
  3.3 1.4 fusion.95
  5.6 11.5 %all-to-all-start.1 = ((s32[128,2,2,128]{3,1,2,0:T(2,128)}), s32[128,2,2,128]{3,1,2,0:T(2,128)S(1)}, u32[]{:S(2)}, u32[]{:S(2)}) async-start(s32[128,2,2,128]{3,1,2,0:T(2,128)} %copy.72), calls=%async_computation.1 | async-start | bytes 524288 | tf_op jit(solution)/shard_map/all_to_all | solution.py:240
  18.1 1.7 copy.70
  19.7 8.4 %all-to-all-done.1 = s32[128,2,2,128]{3,1,2,0:T(2,128)S(1)} async-done(((s32[128,2,2,128]{3,1,2,0:T(2,128)}), s32[128,2,2,128]{3,1,2,0:T(2,128)S(1)}, u32[]{:S(2)}, u32[]{:S(2)}) %all-to-all-start.1) | async-done | bytes 262176 | tf_op jit(solution)/shard_map/all_to_all | solution.py:240
  28.2 4.3 %all-to-all-start = ((f32[128,2,12,128]{3,1,2,0:T(2,128)}), f32[128,2,12,128]{3,1,2,0:T(2,128)S(1)}, u32[]{:S(2)}, u32[]{:S(2)}) async-start(f32[128,2,12,128]{3,1,2,0:T(2,128)} %copy.70), calls=%async_computation | async-start | bytes 3145728 | tf_op jit(solution)/shard_map/all_to_all | solution.py:233
  32.9 24.2 %all-to-all-done = f32[128,2,12,128]{3,1,2,0:T(2,128)S(1)} async-done(((f32[128,2,12,128]{3,1,2,0:T(2,128)}), f32[128,2,12,128]{3,1,2,0:T(2,128)S(1)}, u32[]{:S(2)}, u32[]{:S(2)}) %all-to-all-start) | async-done | bytes 1572896 | tf_op jit(solution)/shard_map/all_to_all | solution.py:233
  57.8 1.4 reshape.3130
  59.2 2.4 %copy.84 = f32[16,12,2048]{2,1,0:T(8,128)S(1)} copy(f32[16,12,2048]{2,0,1:T(8,128)} %reshape.3130) | data formatting | bytes 3145728
  61.5 53.0 %while.34 = (s32[]{:T(128)}, f32[4,9,128]{2,1,0:T(8,128)S(1)}, s32[16,2,2048]{2,1,0:T(2,128)S(1)}, f32[16,12,2048]{2,1,0:T(8,128)S(1)}, f32[3,4]{1,0:T(4,128)S(1...) while((s32[]{:T(128)}, f32[4,9,128]{2,1,0:T(8,128)S(1)}, ...), condition=%wide.region_2.3_spmd.clone.clone, body=%wide.region_1.2_spmd.clone.clone.sunk | while | flops 229608976 | bytes 2810339 | solution.py:159
  114.6 2.3 %collective-permute-start = (f32[4,3,128]{2,0,1:T(4,128)S(1)}, f32[4,3,128]{2,0,1:T(4,128)S(1)}, u32[]{:S(2)}, u32[]{:S(2)}) collective-permute-start(f32[4,3,128]{2,0,1:T(4,128)S(1)} %get-tuple-element.625), channel_id=1, source_target_pairs={{0,8},{8,16},{16,24},{24,32},{32,40},{40,48},{48,56},{56,64},{64,7... | collective-permute-start | bytes 18440 | tf_op jit(solution)/shard_map/ppermute | solution.py:24
  117.7 2.6 %collective-permute-start.1 = (f32[4,2,128]{2,1,0:T(2,128)S(1)}, f32[4,2,128]{2,1,0:T(2,128)S(1)}, u32[]{:S(2)}, u32[]{:S(2)}) collective-permute-start(f32[4,2,128]{2,1,0:T(2,128)S(1)} %get-tuple-element.627), channel_id=1, source_target_pairs={{0,1},{1,2},{2,3},{3,4},{4,5},{5,6},{6,7},{8,9},{9,10},{10,11},{11... | collective-permute-start | bytes 12296 | tf_op jit(solution)/shard_map/ppermute | solution.py:24
  120.4 1.3 collective-permute-done.1
  121.8 2.1 collective-permute-start.2
  123.9 2.8 %collective-permute-done.2 = f32[3,2,128]{2,1,0:T(2,128)S(1)} collective-permute-done((f32[3,2,128]{2,1,0:T(2,128)S(1)}, f32[3,2,128]{2,1,0:T(2,128)S(1)}, u32[]{:S(2)}, u32[]{:S(2)}) %collective-permute-start.2) | collective-permute-done | bytes 3104 | tf_op jit(solution)/shard_map/ppermute | solution.py:24
  126.7 1.5 collective-permute-start.3
  128.2 3.4 %collective-permute-done.3 = f32[3,3,128]{2,1,0:T(4,128)S(1)} collective-permute-done((f32[3,3,128]{2,1,0:T(4,128)S(1)}, f32[3,3,128]{2,1,0:T(4,128)S(1)}, u32[]{:S(2)}, u32[]{:S(2)}) %collective-permute-start.3) | collective-permute-done | bytes 4640 | tf_op jit(solution)/shard_map/ppermute | solution.py:24
  131.7 63.1 %while.33 = (s32[]{:T(128)}, f32[16,9,2048]{2,1,0:T(8,128)}, f32[16,12,2048]{2,1,0:T(8,128)S(1)}, s32[16,2,2048]{2,1,0:T(2,128)S(1)}, f32[3,9,128]{2,1,0:T(8,128...) while((s32[]{:T(128)}, f32[16,9,2048]{2,1,0:T(8,128)}, ...), condition=%wide.region_12.13_spmd.clone.clone, body=%wide.region_3.12_spmd.clone.clone.sunk | while | flops 172451840 | bytes 3264377 | solution.py:204
  132.4 1.1 multiply_reduce_fusion.9
  136.3 1.1 multiply_reduce_fusion.9
  152.1 1.1 multiply_reduce_fusion.9
  175.7 1.1 multiply_reduce_fusion.9
  183.6 1.1 multiply_reduce_fusion.9
  194.8 1.6 reshape.3148
  196.9 29.1 %all_to_all.15 = f32[128,2,9,128]{3,1,2,0:T(2,128)S(1)} all-to-all(f32[128,2,9,128]{3,1,2,0:T(2,128)S(1)} %copy.88), channel_id=1, replica_groups=mesh['gx'=16,'gy'=8] {'gx','gy'}, dimensions={0} | all-to-all | bytes 2359296 | tf_op jit(solution)/shard_map/all_to_all | solution.py:251
  (621 shorter events, 116.8 us)
Async XLA Ops:
  0.6 16.4 %copy-start.2 = (f32[192,3,128]{2,0,1:T(8,128)S(1)}, f32[192,3,128]{2,0,1:T(8,128)}, u32[]{:S(2)}) copy-start(f32[192,3,128]{2,0,1:T(8,128)} %param.18) | copy-start | bytes 884740
  0.6 16.4 %copy-start.1 = (f32[192,3,128]{2,0,1:T(8,128)S(1)}, f32[192,3,128]{2,0,1:T(8,128)}, u32[]{:S(2)}) copy-start(f32[192,3,128]{2,0,1:T(8,128)} %param.19) | copy-start | bytes 884740
  0.7 16.4 %copy-start = (f32[192,6,128]{2,0,1:T(8,128)S(1)}, f32[192,6,128]{2,0,1:T(8,128)}, u32[]{:S(2)}) copy-start(f32[192,6,128]{2,0,1:T(8,128)} %param.20) | copy-start | bytes 1769476
  5.6 22.6 %all-to-all-start.1 = ((s32[128,2,2,128]{3,1,2,0:T(2,128)}), s32[128,2,2,128]{3,1,2,0:T(2,128)S(1)}, u32[]{:S(2)}, u32[]{:S(2)}) async-start(s32[128,2,2,128]{3,1,2,0:T(2,128)} %copy.72), calls=%async_computation.1 | async-start | bytes 524288 | tf_op jit(solution)/shard_map/all_to_all | solution.py:240
  28.2 28.9 %all-to-all-start = ((f32[128,2,12,128]{3,1,2,0:T(2,128)}), f32[128,2,12,128]{3,1,2,0:T(2,128)S(1)}, u32[]{:S(2)}, u32[]{:S(2)}) async-start(f32[128,2,12,128]{3,1,2,0:T(2,128)} %copy.70), calls=%async_computation | async-start | bytes 3145728 | tf_op jit(solution)/shard_map/all_to_all | solution.py:233
  59.2 2.4 %copy-start.3 = (f32[3,4]{1,0:T(4,128)S(1)}, f32[3,4]{1,0:T(4,128)}, u32[]{:S(2)}) copy-start(f32[3,4]{1,0:T(4,128)} %param.25) | copy-start | bytes 148
  114.6 3.1 %collective-permute-start = (f32[4,3,128]{2,0,1:T(4,128)S(1)}, f32[4,3,128]{2,0,1:T(4,128)S(1)}, u32[]{:S(2)}, u32[]{:S(2)}) collective-permute-start(f32[4,3,128]{2,0,1:T(4,128)S(1)} %get-tuple-element.625), channel_id=1, source_target_pairs={{0,8},{8,16},{16,24},{24,32},{32,40},{40,48},{48,56},{56,64},{64,7... | collective-permute-start | bytes 18440 | tf_op jit(solution)/shard_map/ppermute | solution.py:24
  117.7 4.0 %collective-permute-start.1 = (f32[4,2,128]{2,1,0:T(2,128)S(1)}, f32[4,2,128]{2,1,0:T(2,128)S(1)}, u32[]{:S(2)}, u32[]{:S(2)}) collective-permute-start(f32[4,2,128]{2,1,0:T(2,128)S(1)} %get-tuple-element.627), channel_id=1, source_target_pairs={{0,1},{1,2},{2,3},{3,4},{4,5},{5,6},{6,7},{8,9},{9,10},{10,11},{11... | collective-permute-start | bytes 12296 | tf_op jit(solution)/shard_map/ppermute | solution.py:24
  121.8 9.9 %copy-start.4 = (f32[3,2,2,128]{3,2,1,0:T(2,128)}, f32[3,2,2,128]{3,2,1,0:T(2,128)S(1)}, u32[]{:S(2)}) copy-start(f32[3,2,2,128]{3,2,1,0:T(2,128)S(1)} %divide_multiply_fusion) | copy-start | bytes 18436
  121.8 4.9 %collective-permute-start.2 = (f32[3,2,128]{2,1,0:T(2,128)S(1)}, f32[3,2,128]{2,1,0:T(2,128)S(1)}, u32[]{:S(2)}, u32[]{:S(2)}) collective-permute-start(f32[3,2,128]{2,1,0:T(2,128)S(1)} %bitcast.579), channel_id=1, source_target_pairs={{1,0},{2,1},{3,2},{4,3},{5,4},{6,5},{7,6},{9,8},{10,9},{11,10},{12... | collective-permute-start | bytes 9224 | tf_op jit(solution)/shard_map/ppermute | solution.py:24
  126.7 4.9 %collective-permute-start.3 = (f32[3,3,128]{2,1,0:T(4,128)S(1)}, f32[3,3,128]{2,1,0:T(4,128)S(1)}, u32[]{:S(2)}, u32[]{:S(2)}) collective-permute-start(f32[3,3,128]{2,1,0:T(4,128)S(1)} %fusion.107), channel_id=1, source_target_pairs={{8,0},{16,8},{24,16},{32,24},{40,32},{48,40},{56,48},{64,56},{72,6... | collective-permute-start | bytes 13832 | tf_op jit(solution)/shard_map/ppermute | solution.py:24
where the time goes:
time: 229 us
  other arithmetic  58.5 us (26%)
  matrix products  57.8 us (25%)
  waiting for transfers between devices  40.9 us (18%)
  blocking collectives  29.1 us (13%)
  starting transfers between devices  24.3 us (11%)
  local copies, waits for them, and re-layouts  13.7 us (6%)
  loops' own time  3.5 us (2%)
    all_to_all x1, blocking collectives, shards(): lax.all_to_all(results.reshape(devices, capacity, 9, width), ('gx', 'gy')...  29.1 us
    dot_general x32, matrix products, gather_step(): columns = jnp.einsum('kxz,zp->kxp', ext_vel, zone, precision=HIGH)  24.9 us
    dot_general x32, matrix products, scatter_step(): grid = grid + jnp.einsum('qxp,zp->qxz', gathered, zone, precision=HIGH)  24.8 us
    all_to_all x1, waiting for transfers between devices, shards(): lax.all_to_all(send_float.reshape(devices, capacity, 12, width), ('gx', '...  24.2 us
    another operation x80, other arithmetic, gather_step(): results = jnp.stack(new_speed + new_strains, axis=0) * live_float[None]  14.2 us
    sub x80, other arithmetic, scatter_step(): rows.append(weight * masses * speeds[comp] - DT_STEP * VOLUME * force)  11.9 us
    all_to_all x1, starting transfers between devices, shards(): lax.all_to_all(send_int.reshape(devices, capacity, 2, width), ('gx', 'gy'...  11.5 us
    dynamic_update_slice x16, other arithmetic, patch_step(): lax.scan(gather_step, jnp.zeros((), jnp.float32), (float_rows, int_rows))  10.7 us
  transfers between devices with their start and end apart: 6, of which 6 were waited for; matrix products, arithmetic and copies ran while one was open for 1% of the time, Pallas kernels for 0%

commit v1 on v0

v1 whole, which is shorter than its diff:
```python
import functools

import jax
import jax.numpy as jnp
from jax import lax
from jax.experimental import pallas as pl
from jax.experimental.pallas import tpu as pltpu
from jax.sharding import PartitionSpec as P

GX = 16
GY = 8
PY = 4
NZ = 128
NB = 192
DT = 0.25
VOLUME = 0.5
GRAVITY = 1.0
FLOOR = 0.25
MESH = pl.DeviceIdType.MESH
F32 = jnp.float32
BF16 = jnp.bfloat16
VMEM = pl.BlockSpec(memory_space=pltpu.VMEM)
SMEM = pl.BlockSpec(memory_space=pltpu.SMEM)
LIMIT = 48 * 1024 * 1024


def iota(shape, dim):
    return lax.broadcasted_iota(jnp.int32, shape, dim)


def live_mask(counts, group):
    sub = iota((8, 128), 0)
    limit = jnp.zeros((8, 128), jnp.int32)
    for s in range(8):
        limit = jnp.where(sub == s, counts[group * 8 + s], limit)
    return iota((8, 128), 1) < limit


def by_material(params, row, mats):
    value = jnp.where(mats == 1, params[row, 1], params[row, 0])
    value = jnp.where(mats == 2, params[row, 2], value)
    return jnp.where(mats == 3, params[row, 3], value)


def source_rows(counts, params, off, vel, strain, mats, rows, group):
    at = pl.ds(pl.multiple_of(group * 8, 8), 8)
    live = live_mask(counts, group)
    material = mats[at, :]
    mass = jnp.where(live, by_material(params, 0, material), 0.0)
    shear = jnp.where(live, by_material(params, 1, material), 0.0) * (-DT * VOLUME)
    e = [strain[k, at, :] for k in range(6)]
    trace = shear * (e[0] + e[1] + e[2])
    twice = 2.0 * shear
    xx, yy, zz = (twice * e[k] + trace for k in range(3))
    xy, xz, yz = (twice * e[k] for k in range(3, 6))
    fz = off[2, at, :]
    zero = jnp.zeros((8, 128), F32)
    full = [mass] + [mass * vel[k, at, :] for k in range(3)]
    base = group * 192

    def put(row, value):
        rows[pl.ds(base + row, 8, stride=24), :] = value

    for q, sz in enumerate((None, xz, yz, zz)):
        upper = fz * full[q]
        if sz is not None:
            upper = upper + sz
        put(4 + q, upper)
        put(q, full[q] - upper)
    for start, terms in ((8, (None, xx, xy, xz)), (16, (None, xy, yy, yz))):
        for q, term in enumerate(terms):
            if term is None:
                put(start + q, zero)
                put(start + 4 + q, zero)
            else:
                upper = fz * term
                put(start + 4 + q, upper)
                put(start + q, term - upper)


def node_rows(rows, off, cells, block):
    base = pl.multiple_of(block * 24, 8)
    t = rows[pl.ds(base, 8), :]
    sx = rows[pl.ds(base + 8, 8), :]
    sy = rows[pl.ds(base + 16, 8), :]
    fx = jnp.broadcast_to(off[0, pl.ds(block, 1), :], (8, 128))
    fy = jnp.broadcast_to(off[1, pl.ds(block, 1), :], (8, 128))
    cell = jnp.broadcast_to(cells[pl.ds(block, 1), :], (8, 128))
    in_x = cell >= 2 * NZ
    in_y = (cell & NZ) != 0
    u1 = fx * t + sx
    u0 = t - u1
    w1 = fx * sy
    w0 = sy - w1
    c11 = fy * u1 + w1
    c10 = u1 - c11
    c01 = fy * u0 + w0
    c00 = u0 - c01
    d = []
    for low, high in ((c00, c10), (c01, c11)):
        d.append(
            (jnp.where(in_x, 0.0, low), jnp.where(in_x, low, high), jnp.where(in_x, high, 0.0))
        )
    tiles = []
    for i in range(3):
        low, high = d[0][i], d[1][i]
        tiles += [jnp.where(in_y, 0.0, low), jnp.where(in_y, low, high), jnp.where(in_y, high, 0.0)]
    tiles.append(jnp.zeros((8, 128), F32))
    full = jnp.concatenate(tiles, axis=0)
    hi = full.astype(BF16)
    lo = (full - hi.astype(F32)).astype(BF16)
    z = (cell & (NZ - 1)).astype(F32)
    z16 = jnp.concatenate([z, z], axis=0).astype(BF16)
    z_all = jnp.concatenate([z16] * 8, axis=0)
    depth = iota((128, 128), 0).astype(F32).astype(BF16)
    hot = jnp.where(depth == z_all, jnp.ones((), BF16), jnp.zeros((), BF16))
    return hi, lo, hot


def contract(left, right):
    return lax.dot_general(left, right, (((1,), (1,)), ((), ())), preferred_element_type=F32)


def scatter_kernel(dest, counts, params, off, vel, strain, cells, mats, out, rows, acc):
    def clear(x, carry):
        acc[x] = jnp.zeros((17, 8, 128), F32)
        return carry

    lax.fori_loop(0, 33, clear, 0)

    def prepare(group, carry):
        source_rows(counts, params, off, vel, strain, mats, rows, group)
        return carry

    lax.fori_loop(0, NB // 8, prepare, 0)

    def spread(pair, carry):
        for s in range(2):
            block = pair * 2 + s
            hi, lo, hot = node_rows(rows, off, cells, block)
            sums = contract(
                jnp.concatenate([hi, lo], axis=1), jnp.concatenate([hot, hot], axis=1)
            )
            d = dest[block]
            x0 = d // GY * 2
            y0 = d % GY * 2
            for i in range(3):
                for j in range(3):
                    n = i * 3 + j
                    acc[x0 + i, y0 + j] += sums[n * 8 : n * 8 + 8]
        return carry

    lax.fori_loop(0, NB // 2, spread, 0)

    low_half = iota((8, 128), 0) < 4
    above = iota((8, 128), 1) > 0

    def fold(gx, carry):
        for x in range(2):
            for gy in range(GY):
                even = acc[gx * 2 + x, gy * 2]
                odd = acc[gx * 2 + x, gy * 2 + 1]
                first = jnp.where(low_half, even, pltpu.roll(odd, 4, axis=0))
                second = jnp.where(low_half, pltpu.roll(even, 4, axis=0), odd)
                second = jnp.where(above, pltpu.roll(second, 1, axis=1), 0.0)
                out[gy % 2, gx, gy // 2, x] = first + second
        return carry

    lax.fori_loop(0, GX, fold, 0)


def update(total):
    sub = iota((8, 128), 0)
    mass_e = jnp.broadcast_to(total[0:1], (8, 128))
    mass_o = jnp.broadcast_to(total[4:5], (8, 128))
    mass = jnp.where(sub < 4, mass_e, mass_o)
    moved = pltpu.roll(total, 7, axis=0)
    comp = sub % 4
    moved = moved + jnp.where(comp == 2, -DT * GRAVITY, 0.0) * mass
    value = moved / jnp.maximum(mass, FLOOR)
    keep = (comp < 3) & (iota((8, 128), 1) > 0)
    return jnp.where(keep, value, 0.0)


def exchange_kernel(
    part, node_vel, mine, from_sib, summed, landed, sib_send, sib_recv, sum_send, sum_recv,
    vel_send, vel_recv, fwd_send, fwd_recv,
):
    gx = lax.axis_index("gx")
    gy = lax.axis_index("gy")
    core = lax.rem(gy, 2)
    y = gy // 2
    sibling = (gx, gy + 1 - 2 * core)
    chip = gx * PY + y

    def peer(step, dy):
        px = lax.rem(gx + step, GX)
        py = lax.rem(y + dy, PY)
        return px, py, (px, py * 2 + core)

    barrier = pltpu.get_barrier_semaphore()
    pl.semaphore_signal(barrier, inc=1, device_id=sibling, device_id_type=MESH)

    def greet(step, carry):
        for dy in range(PY):
            pl.semaphore_signal(barrier, inc=1, device_id=peer(step, dy)[2], device_id_type=MESH)
        return carry

    lax.fori_loop(1, GX, greet, 0)
    for dy in range(1, PY):
        pl.semaphore_signal(barrier, inc=1, device_id=peer(0, dy)[2], device_id_type=MESH)
    pl.semaphore_wait(barrier, GX * PY)

    def sib_copy(px):
        return pltpu.make_async_remote_copy(
            src_ref=part.at[1 - core, px], dst_ref=from_sib.at[px], send_sem=sib_send.at[px],
            recv_sem=sib_recv.at[px], device_id=sibling, device_id_type=MESH,
        )

    def send_sib(step, carry):
        sib_copy(lax.rem(gx + step, GX)).start()
        return carry

    lax.fori_loop(1, GX + 1, send_sib, 0)

    def sum_copy(step, dy):
        px, py, device = peer(step, dy)
        return pltpu.make_async_remote_copy(
            src_ref=summed.at[px, py], dst_ref=landed.at[chip], send_sem=sum_send,
            recv_sem=sum_recv, device_id=device, device_id_type=MESH,
        )

    def add_sib(step):
        px = lax.rem(gx + step, GX)
        sib_copy(px).wait_recv()
        summed[px] = part[core, px] + from_sib[px]

    def send_sums(step, carry):
        add_sib(step)
        for dy in range(PY):
            sum_copy(step, dy).start()
        return carry

    lax.fori_loop(1, GX, send_sums, 0)
    add_sib(0)
    for dy in range(1, PY):
        sum_copy(0, dy).start()
    landed[chip] = summed[gx, y]

    many = landed.at[pl.ds(0, GX * PY - 1)]
    pltpu.make_async_copy(many, many, sum_recv).wait()
    total = lax.fori_loop(
        0, GX * PY, lambda c, so_far: so_far + landed[c], jnp.zeros((2, 8, 128), F32)
    )
    for x in range(2):
        mine[x] = update(total[x])

    own = pltpu.make_async_copy(mine, node_vel.at[core, gx, y], vel_send.at[1])
    own.start()

    def vel_copy(step, dy):
        px, py, device = peer(step, dy)
        return pltpu.make_async_remote_copy(
            src_ref=mine, dst_ref=node_vel.at[core, gx, y], send_sem=vel_send.at[0],
            recv_sem=vel_recv.at[gx], device_id=device, device_id_type=MESH,
        )

    def send_vel(step, carry):
        for dy in range(PY):
            vel_copy(step, dy).start()
        return carry

    for dy in range(1, PY):
        vel_copy(0, dy).start()
    lax.fori_loop(1, GX, send_vel, 0)
    own.wait()

    def forward(px):
        return pltpu.make_async_remote_copy(
            src_ref=node_vel.at[core, px], dst_ref=node_vel.at[core, px], send_sem=fwd_send.at[px],
            recv_sem=fwd_recv.at[px], device_id=sibling, device_id_type=MESH,
        )

    def pass_on(step, carry):
        px = lax.rem(gx + GX - step, GX)
        here = node_vel.at[core, px]
        pltpu.make_async_copy(here, here, vel_recv.at[px]).wait()
        forward(px).start()
        return carry

    few = node_vel.at[core, gx, pl.ds(0, PY - 1)]
    pltpu.make_async_copy(few, few, vel_recv.at[gx]).wait()
    forward(gx).start()
    lax.fori_loop(1, GX, pass_on, 0)

    def finish(px, carry):
        sib_copy(px).wait_send()
        forward(px).wait()
        return carry

    lax.fori_loop(0, GX, finish, 0)
    pltpu.make_async_copy(many, many, sum_send).wait()
    pltpu.make_async_copy(many, many, vel_send.at[0]).wait()


def gather_kernel(dest, counts, params, off, strain, cells, mats, node_vel, out_vel, out_strain, out_node, table, rows):
    gx = lax.axis_index("gx")
    gy = lax.axis_index("gy")
    for x in range(2):
        own = node_vel[lax.rem(gy, 2), gx, gy // 2, x]
        for y in range(2):
            for c in range(3):
                out_node[c, x, y : y + 1, :] = own[y * 4 + c : y * 4 + c + 1]

    zeros = jnp.zeros((8, 128), F32)
    for y in range(17):
        table[32, y] = zeros

    low_half = iota((8, 128), 0) < 4
    below = iota((8, 128), 1) < NZ - 1

    def build(gx, carry):
        for x in range(2):
            for gy in range(GY):
                level = node_vel[gy % 2, gx, gy // 2, x]
                lifted = jnp.where(below, pltpu.roll(level, NZ - 1, axis=1), 0.0)
                table[gx * 2 + x, gy * 2] = jnp.where(low_half, level, pltpu.roll(lifted, 4, axis=0))
                table[gx * 2 + x, gy * 2 + 1] = jnp.where(low_half, pltpu.roll(level, 4, axis=0), lifted)
            table[gx * 2 + x, 16] = zeros
        return carry

    lax.fori_loop(0, GX, build, 0)

    def one_group(group, carry):
        at = pl.ds(pl.multiple_of(group * 8, 8), 8)
        cell8 = cells[at, :]
        fx8 = off[0, at, :]
        fy8 = off[1, at, :]
        for s in range(8):
            d = dest[group * 8 + s]
            x0 = d // GY * 2
            y0 = d % GY * 2
            cell = jnp.broadcast_to(cell8[s : s + 1], (8, 128))
            fx = jnp.broadcast_to(fx8[s : s + 1], (8, 128))
            fy = jnp.broadcast_to(fy8[s : s + 1], (8, 128))
            z = cell & (NZ - 1)
            in_x = cell >= 2 * NZ
            in_y = (cell & NZ) != 0
            got = [
                [
                    jnp.take_along_axis(table[x0 + i, y0 + j], z, axis=1, mode="promise_in_bounds")
                    for j in range(3)
                ]
                for i in range(3)
            ]
            side = [
                [jnp.where(in_y, got[i][b + 1], got[i][b]) for b in range(2)] for i in range(3)
            ]
            p = [
                [jnp.where(in_x, side[a + 1][b], side[a][b]) for b in range(2)] for a in range(2)
            ]
            dy = [p[a][1] - p[a][0] for a in range(2)]
            ly = [p[a][0] + fy * dy[a] for a in range(2)]
            gx_term = ly[1] - ly[0]
            rows[s * 24 : s * 24 + 8, :] = ly[0] + fx * gx_term
            rows[s * 24 + 8 : s * 24 + 16, :] = gx_term
            rows[s * 24 + 16 : s * 24 + 24, :] = dy[0] + fx * (dy[1] - dy[0])

        def row(r):
            return rows[pl.ds(r, 8, stride=24), :]

        fz = off[2, at, :]
        speed = []
        grads = []
        for c in range(3):
            v0, v1 = row(c), row(4 + c)
            gz = v1 - v0
            speed.append(v0 + fz * gz)
            gx0, gx1 = row(8 + c), row(12 + c)
            gy0, gy1 = row(16 + c), row(20 + c)
            grads.append((gx0 + fz * (gx1 - gx0), gy0 + fz * (gy1 - gy0), gz))
        live = live_mask(counts, group)
        limit = by_material(params, 2, mats[at, :])
        e = [strain[k, at, :] for k in range(6)]
        trial = [e[k] + DT * grads[k][k] for k in range(3)]
        for k, (r, c) in enumerate(((0, 1), (0, 2), (1, 2))):
            trial.append(e[3 + k] + (0.5 * DT) * (grads[r][c] + grads[c][r]))
        mean = (trial[0] + trial[1] + trial[2]) * (1.0 / 3.0)
        dev = [trial[k] - mean for k in range(3)] + trial[3:]
        square = [x * x for x in dev]
        size = jnp.sqrt(
            square[0] + square[1] + square[2] + 2.0 * (square[3] + square[4] + square[5])
        )
        factor = limit / jnp.maximum(size, limit)
        for k in range(3):
            out_vel[k, at, :] = jnp.where(live, speed[k], 0.0)
            out_strain[k, at, :] = jnp.where(live, mean + factor * dev[k], 0.0)
            out_strain[3 + k, at, :] = jnp.where(live, factor * dev[3 + k], 0.0)
        return carry

    lax.fori_loop(0, NB // 8, one_group, 0)


def scatter(dest, counts, params, off, vel, strain, cells, mats):
    return pl.pallas_call(
        scatter_kernel,
        out_shape=jax.ShapeDtypeStruct((2, GX, PY, 2, 8, 128), F32),
        in_specs=[SMEM] * 3 + [VMEM] * 5,
        out_specs=VMEM,
        scratch_shapes=[pltpu.VMEM((NB * 24, 128), F32), pltpu.VMEM((33, 17, 8, 128), F32)],
        compiler_params=pltpu.CompilerParams(vmem_limit_bytes=LIMIT),
        name="scatter",
    )(dest, counts, params, off, vel, strain, cells, mats)


def exchange(part):
    dma = pltpu.SemaphoreType.DMA
    return pl.pallas_call(
        exchange_kernel,
        out_shape=jax.ShapeDtypeStruct((2, GX, PY, 2, 8, 128), F32),
        in_specs=[VMEM],
        out_specs=pl.BlockSpec(memory_space=pl.ANY),
        scratch_shapes=[
            pltpu.VMEM((2, 8, 128), F32),
            pltpu.VMEM((GX, PY, 2, 8, 128), F32),
            pltpu.VMEM((GX, PY, 2, 8, 128), F32),
            pltpu.VMEM((GX * PY, 2, 8, 128), F32),
            dma((GX,)), dma((GX,)), dma, dma, dma((2,)), dma((GX,)), dma((GX,)), dma((GX,)),
        ],
        compiler_params=pltpu.CompilerParams(
            collective_id=0, has_side_effects=True, vmem_limit_bytes=LIMIT
        ),
        name="exchange",
    )(part)


def gather(dest, counts, params, off, strain, cells, mats, node_vel):
    return pl.pallas_call(
        gather_kernel,
        out_shape=(
            jax.ShapeDtypeStruct((3, NB, 128), F32),
            jax.ShapeDtypeStruct((6, NB, 128), F32),
            jax.ShapeDtypeStruct((3, 2, 2, 128), F32),
        ),
        in_specs=[SMEM] * 3 + [VMEM] * 5,
        out_specs=(VMEM, VMEM, VMEM),
        scratch_shapes=[pltpu.VMEM((33, 17, 8, 128), F32), pltpu.VMEM((8 * 24, 128), F32)],
        compiler_params=pltpu.CompilerParams(vmem_limit_bytes=LIMIT),
        name="gather",
    )(dest, counts, params, off, strain, cells, mats, node_vel)


def shards(offsets, velocity, strain, cells, materials, counts, block_dest, material_params):
    off, vel, eps = (jnp.transpose(x, (1, 0, 2)) for x in (offsets, velocity, strain))
    dest = block_dest.reshape(NB)
    part = scatter(dest, counts, material_params, off, vel, eps, cells, materials)
    node_vel = exchange(part)
    new_vel, new_eps, own = gather(
        dest, counts, material_params, off, eps, cells, materials, node_vel
    )
    return jnp.transpose(new_vel, (1, 0, 2)), jnp.transpose(new_eps, (1, 0, 2)), own


def solution(mesh):
    blocks = P(("gx", "gy"), None, None)
    rows = P(("gx", "gy"), None)
    in_specs = (blocks, blocks, blocks, rows, rows, P(("gx", "gy")), rows, P())
    out_specs = (blocks, blocks, P(None, "gx", "gy", None))
    return jax.shard_map(shards, mesh=mesh, in_specs=in_specs, out_specs=out_specs, check_vma=False)
```

time: 229 us -> 68 us (0.30)
  Pallas kernels: 0 us -> 61.6 us
  other arithmetic: 58.5 us -> 0 us
  matrix products: 57.8 us -> 0 us
  waiting for transfers between devices: 40.9 us -> 0 us
  blocking collectives: 29.1 us -> 0 us
  starting transfers between devices: 24.3 us -> 0 us
  local copies, waits for them, and re-layouts: 13.7 us -> 5.46 us
  loops' own time: 3.5 us -> 0 us
    pallas_call x0 -> x3, Pallas kernels: none -> 61.6 us  [the longest x1 32.7 us: exchange(): pl.pallas_call(exchange_kernel, out_shape=jax.ShapeDtypeStruct((2, GX, PY...]
    dot_general x99 -> x0, matrix products: 57.8 us -> none  [the longest x32 24.9 us: gather_step(): columns = jnp.einsum('kxz,zp->kxp', ext_vel, zone, precision=HIGH)]
    all_to_all x2 -> x0, waiting for transfers between devices: 32.6 us -> none  [the longest x1 24.2 us: shards(): lax.all_to_all(send_float.reshape(devices, capacity, 12, width), ('gx', '...]
    all_to_all x1 -> x0, blocking collectives: 29.1 us -> none  [shards(): lax.all_to_all(results.reshape(devices, capacity, 9, width), ('gx', 'gy')...]
    all_to_all x2 -> x0, starting transfers between devices: 15.8 us -> none  [the longest x1 11.5 us: shards(): lax.all_to_all(send_int.reshape(devices, capacity, 2, width), ('gx', 'gy'...]
    another operation x81 -> x0, other arithmetic: 15.2 us -> none  [the longest x80 14.2 us: gather_step(): results = jnp.stack(new_speed + new_strains, axis=0) * live_float[None]]
    sub x81 -> x0, other arithmetic: 11.9 us -> none  [the longest x80 11.9 us: scatter_step(): rows.append(weight * masses * speeds[comp] - DT_STEP * VOLUME * force)]
    dynamic_update_slice x16 -> x0, other arithmetic: 10.7 us -> none  [patch_step(): lax.scan(gather_step, jnp.zeros((), jnp.float32), (float_rows, int_rows))]
  transfers between devices with their start and end apart: 6 -> 0, of which waited for: 6 -> 0; matrix products, arithmetic and copies ran while one was open for 1% -> 0% of each run, Pallas kernels for 0% -> 0%
where the time goes in v1:
time: 68 us; the launch traced here: 67.7 us
  Pallas kernels  61.6 us (91%)
  local copies, waits for them, and re-layouts  5.46 us (8%)
  between operations  0.69 us (1%)
    pallas_call x1, Pallas kernels, exchange(): pl.pallas_call(exchange_kernel, out_shape=jax.ShapeDtypeStruct((2, GX, PY...  32.7 us
    pallas_call x1, Pallas kernels, scatter(): pl.pallas_call(scatter_kernel, out_shape=jax.ShapeDtypeStruct((2, GX, PY,...  20.7 us
    pallas_call x1, Pallas kernels, gather(): pl.pallas_call(gather_kernel, out_shape=(jax.ShapeDtypeStruct((3, NB, 128...  8.12 us
    unnamed x18, local copies, waits for them, and re-layouts  5.46 us

profile of v1, /device:TPU:1, one launch (start us, length us, event | category | flops | bytes accessed | tf_op | source)
XLA Modules:
  0.0 67.7 jit_solution(6792420088754439990)
XLA Ops:
  0.6 0.0 copy-start.8
  0.6 0.0 copy-start.6
  0.7 0.0 copy-start.7
  0.7 0.7 copy-done.8
  1.3 0.0 copy-done.6
  1.3 0.0 copy-done.7
  1.3 0.0 copy-start
  1.3 1.1 %copy-done = f32[192,6,128]{2,0,1:T(8,128)S(1)} copy-done((f32[192,6,128]{2,0,1:T(8,128)S(1)}, f32[192,6,128]{2,0,1:T(8,128)}, u32[]{:S(2)}) %copy-start) | copy-done | bytes 589848
  2.4 0.0 copy-start.2
  2.4 1.0 %copy-done.2 = f32[192,3,128]{2,0,1:T(8,128)S(1)} copy-done((f32[192,3,128]{2,0,1:T(8,128)S(1)}, f32[192,3,128]{2,0,1:T(8,128)}, u32[]{:S(2)}) %copy-start.2) | copy-done | bytes 294936
  3.4 0.0 copy-start.3
  3.4 0.9 %copy-done.3 = s32[192,128]{1,0:T(8,128)S(1)} copy-done((s32[192,128]{1,0:T(8,128)S(1)}, s32[192,128]{1,0:T(8,128)}, u32[]{:S(2)}) %copy-start.3) | copy-done | bytes 98328
  4.3 0.0 copy-start.4
  4.3 0.9 %copy-done.4 = s32[192,128]{1,0:T(8,128)S(1)} copy-done((s32[192,128]{1,0:T(8,128)S(1)}, s32[192,128]{1,0:T(8,128)}, u32[]{:S(2)}) %copy-start.4) | copy-done | bytes 98328
  5.2 0.0 copy-start.5
  5.2 1.0 %copy-done.5 = f32[192,3,128]{2,0,1:T(8,128)S(1)} copy-done((f32[192,3,128]{2,0,1:T(8,128)S(1)}, f32[192,3,128]{2,0,1:T(8,128)}, u32[]{:S(2)}) %copy-start.5) | copy-done | bytes 294936
  6.1 20.7 %scatter.1.part = f32[2,16,4,2,8,128]{5,4,3,2,1,0:T(8,128)S(1)} custom-call(s32[192]{0:T(256)S(1)} %bitcast.11, s32[192]{0:T(256)S(1)} %copy-done.8, f32[3,4]{1,0:T(4,128)S(1)} %copy-done.6, f32[3,192,128]{2,1,0:T(8,128)S(1)} %bitcast.8, f32[3,192,128]{2,1,0:T(8,128)S(1)} %bitcast.10, f32[6,192,128]{2,1,0:T(8,128)S(1)} %bitcast.6, s32[192,128]{1,0:T(8,128)S(1)} %copy-done.3, ...), custom_call_target="tpu_custom_call" | custom-call | tf_op jit(solution)/shard_map/scatter/pallas_call | solution.py:405
  26.8 0.0 copy-start.1
  26.8 32.7 %exchange.1.node_vel = f32[2,16,4,2,8,128]{5,4,3,2,1,0:T(8,128)S(1)} custom-call(f32[2,16,4,2,8,128]{5,4,3,2,1,0:T(8,128)S(1)} %scatter.1.part), custom_call_target="tpu_custom_call" | custom-call | tf_op jit(solution)/shard_map/exchange/pallas_call | solution.py:418
  59.6 0.0 copy-done.1
  59.6 8.1 %gather.1 = (f32[3,192,128]{2,1,0:T(8,128)}, f32[6,192,128]{2,1,0:T(8,128)}, f32[3,2,2,128]{3,2,1,0:T(2,128)}) custom-call(s32[192]{0:T(256)S(1)} %bitcast.12, s32[192]{0:T(256)S(1)} %copy-done.8, f32[3,4]{1,0:T(4,128)S(1)} %copy-done.6, f32[3,192,128]{2,1,0:T(8,128)S(1)} %bitcast.9, f32[6,192,128]{2,1,0:T(8,128)S(1)} %bitcast.7, s32[192,128]{1,0:T(8,128)S(1)} %copy-done.3, ...), custom_call_target="tpu_custom_call" | custom-call | tf_op jit(solution)/shard_map/gather/pallas_call | solution.py:438
Async XLA Ops:
  0.6 0.7 %copy-start.8 = (s32[192]{0:T(256)S(1)}, s32[192]{0:T(256)}, u32[]{:S(2)}) copy-start(s32[192]{0:T(256)} %counts.3) | copy-start | bytes 2308
  0.6 0.7 %copy-start.6 = (f32[3,4]{1,0:T(4,128)S(1)}, f32[3,4]{1,0:T(4,128)}, u32[]{:S(2)}) copy-start(f32[3,4]{1,0:T(4,128)} %params.3) | copy-start | bytes 148
  0.7 0.7 %copy-start.7 = (s32[192,1]{0,1:T(1,128)S(1)}, s32[192,1]{0,1:T(1,128)}, u32[]{:S(2)}) copy-start(s32[192,1]{0,1:T(1,128)} %param.14) | copy-start | bytes 2308
  1.3 1.1 %copy-start = (f32[192,6,128]{2,0,1:T(8,128)S(1)}, f32[192,6,128]{2,0,1:T(8,128)}, u32[]{:S(2)}) copy-start(f32[192,6,128]{2,0,1:T(8,128)} %param.10) | copy-start | bytes 1769476
  2.4 1.0 %copy-start.2 = (f32[192,3,128]{2,0,1:T(8,128)S(1)}, f32[192,3,128]{2,0,1:T(8,128)}, u32[]{:S(2)}) copy-start(f32[192,3,128]{2,0,1:T(8,128)} %param.8) | copy-start | bytes 884740
  3.4 0.9 %copy-start.3 = (s32[192,128]{1,0:T(8,128)S(1)}, s32[192,128]{1,0:T(8,128)}, u32[]{:S(2)}) copy-start(s32[192,128]{1,0:T(8,128)} %cells.3) | copy-start | bytes 294916
  4.3 0.9 %copy-start.4 = (s32[192,128]{1,0:T(8,128)S(1)}, s32[192,128]{1,0:T(8,128)}, u32[]{:S(2)}) copy-start(s32[192,128]{1,0:T(8,128)} %mats.3) | copy-start | bytes 294916
  5.2 1.0 %copy-start.5 = (f32[192,3,128]{2,0,1:T(8,128)S(1)}, f32[192,3,128]{2,0,1:T(8,128)}, u32[]{:S(2)}) copy-start(f32[192,3,128]{2,0,1:T(8,128)} %param.9) | copy-start | bytes 884740
  26.8 32.8 %copy-start.1 = (f32[192,6,128]{2,0,1:T(8,128)S(1)}, f32[192,6,128]{2,0,1:T(8,128)}, u32[]{:S(2)}) copy-start(f32[192,6,128]{2,0,1:T(8,128)} %param.10) | copy-start | bytes 1769476

commit v2 on v1

--- a/solution.py
+++ b/solution.py
@@ -1,5 +1,3 @@
-import functools
-
 import jax
 import jax.numpy as jnp
 from jax import lax
@@ -21,7 +19,10 @@
 BF16 = jnp.bfloat16
 VMEM = pl.BlockSpec(memory_space=pltpu.VMEM)
 SMEM = pl.BlockSpec(memory_space=pltpu.SMEM)
-LIMIT = 48 * 1024 * 1024
+HBM = pl.BlockSpec(memory_space=pltpu.HBM)
+LIMIT = 32 * 1024 * 1024
+EMPTY = NB
+ROWS = 32
 
 
 def iota(shape, dim):
@@ -42,7 +43,7 @@
     return jnp.where(mats == 3, params[row, 3], value)
 
 
-def source_rows(counts, params, off, vel, strain, mats, rows, group):
+def source_rows(counts, params, off, vel, strain, cells, mats, rows, group):
     at = pl.ds(pl.multiple_of(group * 8, 8), 8)
     live = live_mask(counts, group)
     material = mats[at, :]
@@ -56,10 +57,10 @@
     fz = off[2, at, :]
     zero = jnp.zeros((8, 128), F32)
     full = [mass] + [mass * vel[k, at, :] for k in range(3)]
-    base = group * 192
+    base = group * (8 * ROWS)
 
     def put(row, value):
-        rows[pl.ds(base + row, 8, stride=24), :] = value
+        rows[pl.ds(base + row, 8, stride=ROWS), :] = value
 
     for q, sz in enumerate((None, xz, yz, zz)):
         upper = fz * full[q]
@@ -76,18 +77,21 @@
                 upper = fz * term
                 put(start + 4 + q, upper)
                 put(start + q, term - upper)
-
-
-def node_rows(rows, off, cells, block):
-    base = pl.multiple_of(block * 24, 8)
-    t = rows[pl.ds(base, 8), :]
-    sx = rows[pl.ds(base + 8, 8), :]
-    sy = rows[pl.ds(base + 16, 8), :]
-    fx = jnp.broadcast_to(off[0, pl.ds(block, 1), :], (8, 128))
-    fy = jnp.broadcast_to(off[1, pl.ds(block, 1), :], (8, 128))
-    cell = jnp.broadcast_to(cells[pl.ds(block, 1), :], (8, 128))
-    in_x = cell >= 2 * NZ
-    in_y = (cell & NZ) != 0
+    cell = cells[at, :]
+    put(24, off[0, at, :])
+    put(25, off[1, at, :])
+    put(26, (cell & (NZ - 1)).astype(F32))
+    put(27, cell.astype(F32))
+    put(28, (cell & NZ).astype(F32))
+
+
+def node_rows(source):
+    t, sx, sy = source[0:8], source[8:16], source[16:24]
+    fx, fy, z, in_x, in_y = (
+        jnp.broadcast_to(source[24 + k : 25 + k], (8, 128)) for k in range(5)
+    )
+    in_x = in_x >= 2.0 * NZ
+    in_y = in_y > 0.0
     u1 = fx * t + sx
     u0 = t - u1
     w1 = fx * sy
@@ -109,7 +113,6 @@
     full = jnp.concatenate(tiles, axis=0)
     hi = full.astype(BF16)
     lo = (full - hi.astype(F32)).astype(BF16)
-    z = (cell & (NZ - 1)).astype(F32)
     z16 = jnp.concatenate([z, z], axis=0).astype(BF16)
     z_all = jnp.concatenate([z16] * 8, axis=0)
     depth = iota((128, 128), 0).astype(F32).astype(BF16)
@@ -121,52 +124,22 @@
     return lax.dot_general(left, right, (((1,), (1,)), ((), ())), preferred_element_type=F32)
 
 
-def scatter_kernel(dest, counts, params, off, vel, strain, cells, mats, out, rows, acc):
-    def clear(x, carry):
-        acc[x] = jnp.zeros((17, 8, 128), F32)
-        return carry
-
-    lax.fori_loop(0, 33, clear, 0)
-
-    def prepare(group, carry):
-        source_rows(counts, params, off, vel, strain, mats, rows, group)
-        return carry
-
-    lax.fori_loop(0, NB // 8, prepare, 0)
-
-    def spread(pair, carry):
-        for s in range(2):
-            block = pair * 2 + s
-            hi, lo, hot = node_rows(rows, off, cells, block)
-            sums = contract(
-                jnp.concatenate([hi, lo], axis=1), jnp.concatenate([hot, hot], axis=1)
-            )
-            d = dest[block]
-            x0 = d // GY * 2
-            y0 = d % GY * 2
-            for i in range(3):
-                for j in range(3):
-                    n = i * 3 + j
-                    acc[x0 + i, y0 + j] += sums[n * 8 : n * 8 + 8]
-        return carry
-
-    lax.fori_loop(0, NB // 2, spread, 0)
-
-    low_half = iota((8, 128), 0) < 4
-    above = iota((8, 128), 1) > 0
-
-    def fold(gx, carry):
-        for x in range(2):
-            for gy in range(GY):
-                even = acc[gx * 2 + x, gy * 2]
-                odd = acc[gx * 2 + x, gy * 2 + 1]
-                first = jnp.where(low_half, even, pltpu.roll(odd, 4, axis=0))
-                second = jnp.where(low_half, pltpu.roll(even, 4, axis=0), odd)
-                second = jnp.where(above, pltpu.roll(second, 1, axis=1), 0.0)
-                out[gy % 2, gx, gy // 2, x] = first + second
-        return carry
-
-    lax.fori_loop(0, GX, fold, 0)
+def find_blocks(dest):
+    lane = iota((8, 128), 1)
+    none = jnp.full((8, 128), EMPTY, jnp.int32)
+
+    def look(step, found):
+        first, last = found
+        for s in range(8):
+            block = step * 8 + s
+            back = NB - 1 - block
+            last = jnp.where(lane == dest[block], block, last)
+            first = jnp.where(lane == dest[back], back, first)
+        return first, last
+
+    first, last = lax.fori_loop(0, NB // 8, look, (none, none))
+    second = jnp.where(last == first, EMPTY, last)
+    return jnp.where(iota((8, 128), 0) == 0, first, second)
 
 
 def update(total):
@@ -182,9 +155,10 @@
     return jnp.where(keep, value, 0.0)
 
 
-def exchange_kernel(
-    part, node_vel, mine, from_sib, summed, landed, sib_send, sib_recv, sum_send, sum_recv,
-    vel_send, vel_recv, fwd_send, fwd_recv,
+def scatter_kernel(
+    dest, counts, params, off_in, vel_in, strain_in, cells_in, mats_in, node_vel,
+    off, vel, strain, cells, mats, found, blocks, rows, acc, part, for_sib, from_sib, mine, landed,
+    in_sem, found_sem, sib_send, sib_recv, sum_send, sum_recv, vel_send, vel_recv, fwd_send, fwd_recv,
 ):
     gx = lax.axis_index("gx")
     gy = lax.axis_index("gy")
@@ -198,6 +172,21 @@
         py = lax.rem(y + dy, PY)
         return px, py, (px, py * 2 + core)
 
+    loads = [
+        pltpu.make_async_copy(src, dst, in_sem.at[k])
+        for k, (src, dst) in enumerate(
+            (
+                (off_in, off),
+                (vel_in, vel),
+                (strain_in, strain),
+                (mats_in, mats),
+                (cells_in, cells),
+            )
+        )
+    ]
+    for load in loads:
+        load.start()
+
     barrier = pltpu.get_barrier_semaphore()
     pl.semaphore_signal(barrier, inc=1, device_id=sibling, device_id_type=MESH)
 
@@ -209,49 +198,118 @@
     lax.fori_loop(1, GX, greet, 0)
     for dy in range(1, PY):
         pl.semaphore_signal(barrier, inc=1, device_id=peer(0, dy)[2], device_id_type=MESH)
+
+    found[...] = find_blocks(dest)
+    to_scalars = pltpu.make_async_copy(found, blocks, found_sem)
+    to_scalars.start()
+
+    rows[NB * ROWS : (NB + 1) * ROWS, :] = jnp.zeros((ROWS, 128), F32)
+    by_block = rows.reshape(NB + 1, ROWS, 128)
+
+    def clear(x, carry):
+        acc[x] = jnp.zeros((17, 8, 128), F32)
+        return carry
+
+    lax.fori_loop(0, 33, clear, 0)
+    for load in loads:
+        load.wait()
+
+    def prepare(group, carry):
+        source_rows(counts, params, off, vel, strain, cells, mats, rows, group)
+        return carry
+
+    lax.fori_loop(0, NB // 8, prepare, 0)
+    to_scalars.wait()
     pl.semaphore_wait(barrier, GX * PY)
+
+    def spread(px):
+        for gyp in range(GY):
+            left, right = [], []
+            for slot in range(2):
+                hi, lo, hot = node_rows(by_block[blocks[slot, px * GY + gyp]])
+                left += [hi, lo]
+                right += [hot, hot]
+            sums = contract(jnp.concatenate(left, axis=1), jnp.concatenate(right, axis=1))
+            for i in range(3):
+                for j in range(3):
+                    n = i * 3 + j
+                    acc[px * 2 + i, gyp * 2 + j] += sums[n * 8 : n * 8 + 8]
+
+    low_half = iota((8, 128), 0) < 4
+    above = iota((8, 128), 1) > 0
+
+    def fold(px):
+        for x in range(2):
+            for yp in range(PY):
+                both = []
+                for c in range(2):
+                    even = acc[px * 2 + x, yp * 4 + c * 2]
+                    odd = acc[px * 2 + x, yp * 4 + c * 2 + 1]
+                    first = jnp.where(low_half, even, pltpu.roll(odd, 4, axis=0))
+                    second = jnp.where(low_half, pltpu.roll(even, 4, axis=0), odd)
+                    second = jnp.where(above, pltpu.roll(second, 1, axis=1), 0.0)
+                    both.append(first + second)
+                part[px, yp, x] = jnp.where(core == 0, both[0], both[1])
+                for_sib[px, yp, x] = jnp.where(core == 0, both[1], both[0])
 
     def sib_copy(px):
         return pltpu.make_async_remote_copy(
-            src_ref=part.at[1 - core, px], dst_ref=from_sib.at[px], send_sem=sib_send.at[px],
+            src_ref=for_sib.at[px], dst_ref=from_sib.at[px], send_sem=sib_send.at[px],
             recv_sem=sib_recv.at[px], device_id=sibling, device_id_type=MESH,
         )
-
-    def send_sib(step, carry):
-        sib_copy(lax.rem(gx + step, GX)).start()
-        return carry
-
-    lax.fori_loop(1, GX + 1, send_sib, 0)
 
     def sum_copy(step, dy):
         px, py, device = peer(step, dy)
         return pltpu.make_async_remote_copy(
-            src_ref=summed.at[px, py], dst_ref=landed.at[chip], send_sem=sum_send,
+            src_ref=part.at[px, py], dst_ref=landed.at[chip], send_sem=sum_send,
             recv_sem=sum_recv, device_id=device, device_id_type=MESH,
         )
 
     def add_sib(step):
         px = lax.rem(gx + step, GX)
         sib_copy(px).wait_recv()
-        summed[px] = part[core, px] + from_sib[px]
-
-    def send_sums(step, carry):
+        part[px] = part[px] + from_sib[px]
+
+    def send_sums(step):
         add_sib(step)
         for dy in range(PY):
             sum_copy(step, dy).start()
-        return carry
-
-    lax.fori_loop(1, GX, send_sums, 0)
+
+    def finish_chunk(px):
+        fold(px)
+        sib_copy(px).start()
+
+    def chunk(step, carry):
+        px = lax.rem(gx + step, GX)
+        spread(px)
+
+        @pl.when(step > 0)
+        def _():
+            finish_chunk(px)
+
+        @pl.when(step > 1)
+        def _():
+            send_sums(step - 1)
+
+        return carry
+
+    lax.fori_loop(0, GX, chunk, 0)
+    finish_chunk(gx)
+    send_sums(GX - 1)
     add_sib(0)
     for dy in range(1, PY):
         sum_copy(0, dy).start()
-    landed[chip] = summed[gx, y]
+    landed[chip] = part[gx, y]
 
     many = landed.at[pl.ds(0, GX * PY - 1)]
     pltpu.make_async_copy(many, many, sum_recv).wait()
-    total = lax.fori_loop(
-        0, GX * PY, lambda c, so_far: so_far + landed[c], jnp.zeros((2, 8, 128), F32)
-    )
+
+    def add_up(c, so_far):
+        for k in range(8):
+            so_far = so_far + landed[c * 8 + k]
+        return so_far
+
+    total = lax.fori_loop(0, GX * PY // 8, add_up, jnp.zeros((2, 8, 128), F32))
     for x in range(2):
         mine[x] = update(total[x])
 
@@ -270,9 +328,9 @@
             vel_copy(step, dy).start()
         return carry
 
+    lax.fori_loop(1, GX, send_vel, 0)
     for dy in range(1, PY):
         vel_copy(0, dy).start()
-    lax.fori_loop(1, GX, send_vel, 0)
     own.wait()
 
     def forward(px):
@@ -402,36 +460,34 @@
 
 
 def scatter(dest, counts, params, off, vel, strain, cells, mats):
+    dma = pltpu.SemaphoreType.DMA
+    chunks = pltpu.VMEM((GX, PY, 2, 8, 128), F32)
     return pl.pallas_call(
         scatter_kernel,
         out_shape=jax.ShapeDtypeStruct((2, GX, PY, 2, 8, 128), F32),
-        in_specs=[SMEM] * 3 + [VMEM] * 5,
-        out_specs=VMEM,
-        scratch_shapes=[pltpu.VMEM((NB * 24, 128), F32), pltpu.VMEM((33, 17, 8, 128), F32)],
-        compiler_params=pltpu.CompilerParams(vmem_limit_bytes=LIMIT),
+        in_specs=[SMEM] * 3 + [HBM] * 5,
+        out_specs=pl.BlockSpec(memory_space=pl.ANY),
+        scratch_shapes=[
+            pltpu.VMEM((3, NB, 128), F32),
+            pltpu.VMEM((3, NB, 128), F32),
+            pltpu.VMEM((6, NB, 128), F32),
+            pltpu.VMEM((NB, 128), jnp.int32),
+            pltpu.VMEM((NB, 128), jnp.int32),
+            pltpu.VMEM((8, 128), jnp.int32),
+            pltpu.SMEM((8, 128), jnp.int32),
+            pltpu.VMEM(((NB + 1) * ROWS, 128), F32),
+            pltpu.VMEM((33, 17, 8, 128), F32),
+            chunks, chunks, chunks,
+            pltpu.VMEM((2, 8, 128), F32),
+            pltpu.VMEM((GX * PY, 2, 8, 128), F32),
+            dma((5,)), dma, dma((GX,)), dma((GX,)), dma, dma, dma((2,)), dma((GX,)), dma((GX,)),
+            dma((GX,)),
+        ],
+        compiler_params=pltpu.CompilerParams(
+            collective_id=0, has_side_effects=True, vmem_limit_bytes=60 * 1024 * 1024
+        ),
         name="scatter",
     )(dest, counts, params, off, vel, strain, cells, mats)
-
-
-def exchange(part):
-    dma = pltpu.SemaphoreType.DMA
-    return pl.pallas_call(
-        exchange_kernel,
-        out_shape=jax.ShapeDtypeStruct((2, GX, PY, 2, 8, 128), F32),
-        in_specs=[VMEM],
-        out_specs=pl.BlockSpec(memory_space=pl.ANY),
-        scratch_shapes=[
-            pltpu.VMEM((2, 8, 128), F32),
-            pltpu.VMEM((GX, PY, 2, 8, 128), F32),
-            pltpu.VMEM((GX, PY, 2, 8, 128), F32),
-            pltpu.VMEM((GX * PY, 2, 8, 128), F32),
-            dma((GX,)), dma((GX,)), dma, dma, dma((2,)), dma((GX,)), dma((GX,)), dma((GX,)),
-        ],
-        compiler_params=pltpu.CompilerParams(
-            collective_id=0, has_side_effects=True, vmem_limit_bytes=LIMIT
-        ),
-        name="exchange",
-    )(part)
 
 
 def gather(dest, counts, params, off, strain, cells, mats, node_vel):
@@ -453,8 +509,7 @@
 def shards(offsets, velocity, strain, cells, materials, counts, block_dest, material_params):
     off, vel, eps = (jnp.transpose(x, (1, 0, 2)) for x in (offsets, velocity, strain))
     dest = block_dest.reshape(NB)
-    part = scatter(dest, counts, material_params, off, vel, eps, cells, materials)
-    node_vel = exchange(part)
+    node_vel = scatter(dest, counts, material_params, off, vel, eps, cells, materials)
     new_vel, new_eps, own = gather(
         dest, counts, material_params, off, eps, cells, materials, node_vel
     )

time: 68 us -> 50.4 us (0.74)
  Pallas kernels: 61.6 us -> 48.3 us
  local copies, waits for them, and re-layouts: 5.46 us -> 1.25 us
    pallas_call x1 -> x0, Pallas kernels: 32.7 us -> none  [exchange(): pl.pallas_call(exchange_kernel, out_shape=jax.ShapeDtypeStruct((2, GX, PY...]
    pallas_call x1, Pallas kernels: 20.7 us -> 40.1 us  [scatter(): pl.pallas_call(scatter_kernel, out_shape=jax.ShapeDtypeStruct((2, GX, PY,...]
    unnamed x18 -> x16, local copies, waits for them, and re-layouts: 5.46 us -> 1.25 us
where the time goes in v2:
time: 50.4 us; the launch traced here: 50.3 us
  Pallas kernels  48.3 us (96%)
  local copies, waits for them, and re-layouts  1.25 us (2%)
  between operations  0.76 us (2%)
    pallas_call x1, Pallas kernels, scatter(): pl.pallas_call(scatter_kernel, out_shape=jax.ShapeDtypeStruct((2, GX, PY,...  40.1 us
    pallas_call x1, Pallas kernels, gather(): pl.pallas_call(gather_kernel, out_shape=(jax.ShapeDtypeStruct((3, NB, 128...  8.12 us
    unnamed x16, local copies, waits for them, and re-layouts  1.25 us

profile of v2, /device:TPU:1, one launch (start us, length us, event | category | flops | bytes accessed | tf_op | source)
XLA Modules:
  0.0 50.3 jit_solution(13262173274767167605)
XLA Ops:
  0.6 0.0 copy-start.1
  0.6 0.0 copy-start.2
  0.7 0.0 copy-start.3
  0.7 0.0 copy-start.4
  0.7 0.0 copy-start.5
  0.7 0.0 copy-start.6
  0.7 0.0 copy-start.7
  0.7 40.1 %scatter.1.node_vel = f32[2,16,4,2,8,128]{5,4,3,2,1,0:T(8,128)} custom-call(s32[192]{0:T(256)} %bitcast.10, s32[192]{0:T(256)} %counts.3, f32[3,4]{1,0:T(4,128)} %params.3, f32[3,192,128]{2,1,0:T(8,128)} %bitcast.8, f32[3,192,128]{2,1,0:T(8,128)} %bitcast.12, f32[6,192,128]{2,1,0:T(8,128)} %bitcast.6, s32[192,128]{1,0:T(8,128)} %cells.1, s32[192,128]{1,0:T(8,128)} %mats.1), custom_call_target="tpu_custom_call" | custom-call | tf_op jit(solution)/shard_map/scatter/pallas_call | solution.py:465
  40.9 0.0 copy-done.1
  40.9 0.0 copy-done.2
  40.9 0.0 copy-done.3
  40.9 0.0 copy-done.4
  40.9 0.0 copy-done.5
  40.9 0.0 copy-done.6
  40.9 0.0 copy-done.7
  40.9 0.0 copy-start
  40.9 1.2 %copy-done = f32[2,16,4,2,8,128]{5,4,3,2,1,0:T(8,128)S(1)} copy-done((f32[2,16,4,2,8,128]{5,4,3,2,1,0:T(8,128)S(1)}, f32[2,16,4,2,8,128]{5,4,3,2,1,0:T(8,128)}, u32[]{:S(2)}) %copy-start) | copy-done | bytes 1048600
  42.2 8.1 %gather.1 = (f32[3,192,128]{2,1,0:T(8,128)}, f32[6,192,128]{2,1,0:T(8,128)}, f32[3,2,2,128]{3,2,1,0:T(2,128)}) custom-call(s32[192]{0:T(256)S(1)} %bitcast.11, s32[192]{0:T(256)S(1)} %copy-done.7, f32[3,4]{1,0:T(4,128)S(1)} %copy-done.5, f32[3,192,128]{2,1,0:T(8,128)S(1)} %bitcast.9, f32[6,192,128]{2,1,0:T(8,128)S(1)} %bitcast.7, s32[192,128]{1,0:T(8,128)S(1)} %copy-done.3, ...), custom_call_target="tpu_custom_call" | custom-call | tf_op jit(solution)/shard_map/gather/pallas_call | solution.py:494
Async XLA Ops:
  0.6 40.2 %copy-start.1 = (f32[192,6,128]{2,0,1:T(8,128)S(1)}, f32[192,6,128]{2,0,1:T(8,128)}, u32[]{:S(2)}) copy-start(f32[192,6,128]{2,0,1:T(8,128)} %param.10) | copy-start | bytes 1769476
  0.6 40.2 %copy-start.2 = (f32[192,3,128]{2,0,1:T(8,128)S(1)}, f32[192,3,128]{2,0,1:T(8,128)}, u32[]{:S(2)}) copy-start(f32[192,3,128]{2,0,1:T(8,128)} %param.8) | copy-start | bytes 884740
  0.7 40.2 %copy-start.3 = (s32[192,128]{1,0:T(8,128)S(1)}, s32[192,128]{1,0:T(8,128)}, u32[]{:S(2)}) copy-start(s32[192,128]{1,0:T(8,128)} %cells.1) | copy-start | bytes 294916
  0.7 40.2 %copy-start.4 = (s32[192,128]{1,0:T(8,128)S(1)}, s32[192,128]{1,0:T(8,128)}, u32[]{:S(2)}) copy-start(s32[192,128]{1,0:T(8,128)} %mats.1) | copy-start | bytes 294916
  0.7 40.2 %copy-start.5 = (f32[3,4]{1,0:T(4,128)S(1)}, f32[3,4]{1,0:T(4,128)}, u32[]{:S(2)}) copy-start(f32[3,4]{1,0:T(4,128)} %params.3) | copy-start | bytes 148
  0.7 40.2 %copy-start.6 = (s32[192,1]{0,1:T(1,128)S(1)}, s32[192,1]{0,1:T(1,128)}, u32[]{:S(2)}) copy-start(s32[192,1]{0,1:T(1,128)} %param.14) | copy-start | bytes 2308
  0.7 40.2 %copy-start.7 = (s32[192]{0:T(256)S(1)}, s32[192]{0:T(256)}, u32[]{:S(2)}) copy-start(s32[192]{0:T(256)} %counts.3) | copy-start | bytes 2308
  40.9 1.2 %copy-start = (f32[2,16,4,2,8,128]{5,4,3,2,1,0:T(8,128)S(1)}, f32[2,16,4,2,8,128]{5,4,3,2,1,0:T(8,128)}, u32[]{:S(2)}) copy-start(f32[2,16,4,2,8,128]{5,4,3,2,1,0:T(8,128)} %scatter.1.node_vel) | copy-start | bytes 3145732

commit v3 on v2

--- a/solution.py
+++ b/solution.py
@@ -20,9 +20,16 @@
 VMEM = pl.BlockSpec(memory_space=pltpu.VMEM)
 SMEM = pl.BlockSpec(memory_space=pltpu.SMEM)
 HBM = pl.BlockSpec(memory_space=pltpu.HBM)
-LIMIT = 32 * 1024 * 1024
+LIMIT = 60 * 1024 * 1024
 EMPTY = NB
 ROWS = 32
+LAG = 3
+FIRST = 12
+UNROLL = 4
+FAR_FIRST = sorted(
+    ((dz, dx, dy) for dz in range(4) for dx in range(4) for dy in range(4) if dz + dx + dy),
+    key=lambda o: -sum(min(d, 4 - d) for d in o),
+)
 
 
 def iota(shape, dim):
@@ -83,6 +90,7 @@
     put(26, (cell & (NZ - 1)).astype(F32))
     put(27, cell.astype(F32))
     put(28, (cell & NZ).astype(F32))
+    put(29, fz)
 
 
 def node_rows(source):
@@ -156,9 +164,11 @@
 
 
 def scatter_kernel(
-    dest, counts, params, off_in, vel_in, strain_in, cells_in, mats_in, node_vel,
+    dest, counts, params, off_in, vel_in, strain_in, cells_in, mats_in, slots_out, found_out, mine_out,
     off, vel, strain, cells, mats, found, blocks, rows, acc, part, for_sib, from_sib, mine, landed,
+    node_vel, table, slots,
     in_sem, found_sem, sib_send, sib_recv, sum_send, sum_recv, vel_send, vel_recv, fwd_send, fwd_recv,
+    out_sem, small_sem,
 ):
     gx = lax.axis_index("gx")
     gy = lax.axis_index("gy")
@@ -202,6 +212,8 @@
     found[...] = find_blocks(dest)
     to_scalars = pltpu.make_async_copy(found, blocks, found_sem)
     to_scalars.start()
+    found_copy = pltpu.make_async_copy(found, found_out, small_sem.at[0])
+    found_copy.start()
 
     rows[NB * ROWS : (NB + 1) * ROWS, :] = jnp.zeros((ROWS, 128), F32)
     by_block = rows.reshape(NB + 1, ROWS, 128)
@@ -211,6 +223,10 @@
         return carry
 
     lax.fori_loop(0, 33, clear, 0)
+    for x in range(33):
+        table[x, 16] = jnp.zeros((8, 128), F32)
+    for yn in range(16):
+        table[32, yn] = jnp.zeros((8, 128), F32)
     for load in loads:
         load.wait()
 
@@ -220,7 +236,6 @@
 
     lax.fori_loop(0, NB // 8, prepare, 0)
     to_scalars.wait()
-    pl.semaphore_wait(barrier, GX * PY)
 
     def spread(px):
         for gyp in range(GY):
@@ -283,19 +298,24 @@
         px = lax.rem(gx + step, GX)
         spread(px)
 
+        @pl.when(step == 1)
+        def _():
+            pl.semaphore_wait(barrier, GX * PY)
+
         @pl.when(step > 0)
         def _():
             finish_chunk(px)
 
-        @pl.when(step > 1)
+        @pl.when(step > LAG)
         def _():
-            send_sums(step - 1)
+            send_sums(step - LAG)
 
         return carry
 
     lax.fori_loop(0, GX, chunk, 0)
     finish_chunk(gx)
-    send_sums(GX - 1)
+    for step in range(GX - LAG, GX):
+        send_sums(step)
     add_sib(0)
     for dy in range(1, PY):
         sum_copy(0, dy).start()
@@ -311,27 +331,24 @@
 
     total = lax.fori_loop(0, GX * PY // 8, add_up, jnp.zeros((2, 8, 128), F32))
     for x in range(2):
-        mine[x] = update(total[x])
-
-    own = pltpu.make_async_copy(mine, node_vel.at[core, gx, y], vel_send.at[1])
-    own.start()
-
-    def vel_copy(step, dy):
-        px, py, device = peer(step, dy)
-        return pltpu.make_async_remote_copy(
-            src_ref=mine, dst_ref=node_vel.at[core, gx, y], send_sem=vel_send.at[0],
-            recv_sem=vel_recv.at[gx], device_id=device, device_id_type=MESH,
-        )
-
-    def send_vel(step, carry):
-        for dy in range(PY):
-            vel_copy(step, dy).start()
-        return carry
-
-    lax.fori_loop(1, GX, send_vel, 0)
-    for dy in range(1, PY):
-        vel_copy(0, dy).start()
-    own.wait()
+        value = update(total[x])
+        for yn in range(2):
+            for c in range(3):
+                mine[c, x * 2 + yn : x * 2 + yn + 1, :] = value[yn * 4 + c : yn * 4 + c + 1]
+
+    z, x4 = gx // 4, lax.rem(gx, 4)
+    turn = 1 - 2 * core
+    for dz, dx, dy in FAR_FIRST:
+        pz = lax.rem(z + turn * dz + 4, 4)
+        px = lax.rem(x4 + turn * dx + 4, 4)
+        py = lax.rem(y + turn * dy + 4, 4)
+        pltpu.make_async_remote_copy(
+            src_ref=mine, dst_ref=node_vel.at[core, gx, y], send_sem=vel_send,
+            recv_sem=vel_recv.at[gx], device_id=(pz * 4 + px, py * 2 + core), device_id_type=MESH,
+        ).start()
+    node_vel[core, gx, y] = mine[...]
+    mine_copy = pltpu.make_async_copy(mine, mine_out, small_sem.at[1])
+    mine_copy.start()
 
     def forward(px):
         return pltpu.make_async_remote_copy(
@@ -339,104 +356,162 @@
             recv_sem=fwd_recv.at[px], device_id=sibling, device_id_type=MESH,
         )
 
-    def pass_on(step, carry):
-        px = lax.rem(gx + GX - step, GX)
-        here = node_vel.at[core, px]
-        pltpu.make_async_copy(here, here, vel_recv.at[px]).wait()
+    def order(step):
+        return lax.rem(gx + (FIRST + step), GX)
+
+    def pass_on(step):
+        px = order(step)
+
+        @pl.when(step == GX - FIRST)
+        def _():
+            few = node_vel.at[core, px, pl.ds(0, PY - 1)]
+            pltpu.make_async_copy(few, few, vel_recv.at[px]).wait()
+
+        @pl.when(step != GX - FIRST)
+        def _():
+            here = node_vel.at[core, px]
+            pltpu.make_async_copy(here, here, vel_recv.at[px]).wait()
+
         forward(px).start()
+
+    sub = iota((8, 128), 0)
+    below = iota((8, 128), 1) < NZ - 1
+
+    def build(step):
+        px = order(step)
+        forward(px).wait_recv()
+        for x in range(2):
+            for yn in range(2 * GY):
+                gyp = yn // 2
+                n = x * 2 + yn % 2
+                c0, c1, c2 = (
+                    jnp.broadcast_to(node_vel[gyp % 2, px, gyp // 2, c, n : n + 1, :], (8, 128))
+                    for c in range(3)
+                )
+                level = jnp.where(sub % 4 == 0, c0, jnp.where(sub % 4 == 1, c1, c2))
+                lifted = jnp.where(below, pltpu.roll(level, NZ - 1, axis=1), 0.0)
+                table[px * 2 + x, yn] = jnp.where(low_half, level, lifted)
+
+    def pick(px):
+        for gyp in range(GY):
+            tiles = [[table[px * 2 + i, gyp * 2 + j] for j in range(3)] for i in range(3)]
+            for slot in range(2):
+                patch = px * GY + gyp
+                misc = by_block[blocks[slot, patch], 24:32, :]
+                fx, fy, cz, in_x, in_y, fz = (
+                    jnp.broadcast_to(misc[k : k + 1], (8, 128)) for k in range(6)
+                )
+                cz = cz.astype(jnp.int32)
+                in_x = in_x >= 2.0 * NZ
+                in_y = in_y > 0.0
+                got = [
+                    [
+                        jnp.take_along_axis(tile, cz, axis=1, mode="promise_in_bounds")
+                        for tile in line
+                    ]
+                    for line in tiles
+                ]
+                side = [
+                    [jnp.where(in_y, line[b + 1], line[b]) for b in range(2)] for line in got
+                ]
+                p = [
+                    [jnp.where(in_x, side[a + 1][b], side[a][b]) for b in range(2)]
+                    for a in range(2)
+                ]
+                dy = [p[a][1] - p[a][0] for a in range(2)]
+                ly = [p[a][0] + fy * dy[a] for a in range(2)]
+                dx = ly[1] - ly[0]
+                value = ly[0] + fx * dx
+                dy = dy[0] + fx * (dy[1] - dy[0])
+                part_z = jnp.where(low_half, fz, 1.0 - fz)
+                dz = pltpu.roll(value, 4, axis=0) - value
+                value = value + part_z * dz
+                dx = dx + part_z * (pltpu.roll(dx, 4, axis=0) - dx)
+                dy = dy + part_z * (pltpu.roll(dy, 4, axis=0) - dy)
+                slots[patch * 2 + slot, 0:8, :] = jnp.where(low_half, value, dz)
+                slots[patch * 2 + slot, 8:16, :] = jnp.where(low_half, dx, dy)
+
+    def slots_copy(px):
+        at = pl.ds(px * (2 * GY), 2 * GY)
+        return pltpu.make_async_copy(slots.at[at], slots_out.at[at], out_sem.at[px])
+
+    pass_on(0)
+    pass_on(1)
+    build(0)
+
+    def gather_chunk(step, carry):
+        @pl.when(step < GX - 2)
+        def _():
+            pass_on(step + 2)
+
+        @pl.when(step < GX - 1)
+        def _():
+            build(step + 1)
+
+        pick(order(step))
+        slots_copy(order(step)).start()
         return carry
 
-    few = node_vel.at[core, gx, pl.ds(0, PY - 1)]
-    pltpu.make_async_copy(few, few, vel_recv.at[gx]).wait()
-    forward(gx).start()
-    lax.fori_loop(1, GX, pass_on, 0)
+    lax.fori_loop(0, GX, gather_chunk, 0)
 
     def finish(px, carry):
         sib_copy(px).wait_send()
-        forward(px).wait()
+        forward(px).wait_send()
+        slots_copy(px).wait()
         return carry
 
     lax.fori_loop(0, GX, finish, 0)
     pltpu.make_async_copy(many, many, sum_send).wait()
-    pltpu.make_async_copy(many, many, vel_send.at[0]).wait()
-
-
-def gather_kernel(dest, counts, params, off, strain, cells, mats, node_vel, out_vel, out_strain, out_node, table, rows):
-    gx = lax.axis_index("gx")
-    gy = lax.axis_index("gy")
+    own_vel = node_vel.at[core, pl.ds(0, GX - 1)]
+    pltpu.make_async_copy(own_vel, own_vel, vel_send).wait()
+    own_few = node_vel.at[core, 0, pl.ds(0, PY - 1)]
+    pltpu.make_async_copy(own_few, own_few, vel_send).wait()
+    found_copy.wait()
+    mine_copy.wait()
+
+
+def strain_kernel(
+    dest_in, counts_in, params, found_in, strain_in, mats_in, slots_in, mine_in,
+    out_vel, out_strain, out_node,
+    lines, dest, counts, found, strain, mats, slots, mine, in_sem,
+):
+    loads = [
+        pltpu.make_async_copy(src, dst, in_sem.at[k])
+        for k, (src, dst) in enumerate(
+            (
+                (slots_in, slots),
+                (strain_in, strain),
+                (mats_in, mats),
+                (dest_in, dest),
+                (counts_in, counts),
+                (found_in, found),
+                (mine_in, mine),
+            )
+        )
+    ]
+    for load in loads:
+        load.start()
+    for load in loads:
+        load.wait()
+
     for x in range(2):
-        own = node_vel[lax.rem(gy, 2), gx, gy // 2, x]
-        for y in range(2):
+        for yn in range(2):
             for c in range(3):
-                out_node[c, x, y : y + 1, :] = own[y * 4 + c : y * 4 + c + 1]
-
-    zeros = jnp.zeros((8, 128), F32)
-    for y in range(17):
-        table[32, y] = zeros
-
-    low_half = iota((8, 128), 0) < 4
-    below = iota((8, 128), 1) < NZ - 1
-
-    def build(gx, carry):
-        for x in range(2):
-            for gy in range(GY):
-                level = node_vel[gy % 2, gx, gy // 2, x]
-                lifted = jnp.where(below, pltpu.roll(level, NZ - 1, axis=1), 0.0)
-                table[gx * 2 + x, gy * 2] = jnp.where(low_half, level, pltpu.roll(lifted, 4, axis=0))
-                table[gx * 2 + x, gy * 2 + 1] = jnp.where(low_half, pltpu.roll(level, 4, axis=0), lifted)
-            table[gx * 2 + x, 16] = zeros
-        return carry
-
-    lax.fori_loop(0, GX, build, 0)
-
-    def one_group(group, carry):
+                out_node[c, x, yn : yn + 1, :] = mine[c, x * 2 + yn : x * 2 + yn + 1, :]
+
+    def one_group(group, lane):
         at = pl.ds(pl.multiple_of(group * 8, 8), 8)
-        cell8 = cells[at, :]
-        fx8 = off[0, at, :]
-        fy8 = off[1, at, :]
         for s in range(8):
-            d = dest[group * 8 + s]
-            x0 = d // GY * 2
-            y0 = d % GY * 2
-            cell = jnp.broadcast_to(cell8[s : s + 1], (8, 128))
-            fx = jnp.broadcast_to(fx8[s : s + 1], (8, 128))
-            fy = jnp.broadcast_to(fy8[s : s + 1], (8, 128))
-            z = cell & (NZ - 1)
-            in_x = cell >= 2 * NZ
-            in_y = (cell & NZ) != 0
-            got = [
-                [
-                    jnp.take_along_axis(table[x0 + i, y0 + j], z, axis=1, mode="promise_in_bounds")
-                    for j in range(3)
-                ]
-                for i in range(3)
-            ]
-            side = [
-                [jnp.where(in_y, got[i][b + 1], got[i][b]) for b in range(2)] for i in range(3)
-            ]
-            p = [
-                [jnp.where(in_x, side[a + 1][b], side[a][b]) for b in range(2)] for a in range(2)
-            ]
-            dy = [p[a][1] - p[a][0] for a in range(2)]
-            ly = [p[a][0] + fy * dy[a] for a in range(2)]
-            gx_term = ly[1] - ly[0]
-            rows[s * 24 : s * 24 + 8, :] = ly[0] + fx * gx_term
-            rows[s * 24 + 8 : s * 24 + 16, :] = gx_term
-            rows[s * 24 + 16 : s * 24 + 24, :] = dy[0] + fx * (dy[1] - dy[0])
+            block = group * 8 + s
+            d = dest[block]
+            slot = d * 2 + jnp.where(found[0, d] == block, 0, 1)
+            lines[lane * 128 + s * 16 : lane * 128 + s * 16 + 16, :] = slots[slot]
 
         def row(r):
-            return rows[pl.ds(r, 8, stride=24), :]
-
-        fz = off[2, at, :]
-        speed = []
-        grads = []
-        for c in range(3):
-            v0, v1 = row(c), row(4 + c)
-            gz = v1 - v0
-            speed.append(v0 + fz * gz)
-            gx0, gx1 = row(8 + c), row(12 + c)
-            gy0, gy1 = row(16 + c), row(20 + c)
-            grads.append((gx0 + fz * (gx1 - gx0), gy0 + fz * (gy1 - gy0), gz))
+            return lines[pl.ds(lane * 128 + r, 8, stride=16), :]
+
+        speed = [row(c) for c in range(3)]
+        grads = [(row(8 + c), row(12 + c), -row(4 + c)) for c in range(3)]
         live = live_mask(counts, group)
         limit = by_material(params, 2, mats[at, :])
         e = [strain[k, at, :] for k in range(6)]
@@ -454,9 +529,13 @@
             out_vel[k, at, :] = jnp.where(live, speed[k], 0.0)
             out_strain[k, at, :] = jnp.where(live, mean + factor * dev[k], 0.0)
             out_strain[3 + k, at, :] = jnp.where(live, factor * dev[3 + k], 0.0)
+
+    def groups(step, carry):
+        for lane in range(UNROLL):
+            one_group(step * UNROLL + lane, lane)
         return carry
 
-    lax.fori_loop(0, NB // 8, one_group, 0)
+    lax.fori_loop(0, NB // 8 // UNROLL, groups, 0)
 
 
 def scatter(dest, counts, params, off, vel, strain, cells, mats):
@@ -464,9 +543,13 @@
     chunks = pltpu.VMEM((GX, PY, 2, 8, 128), F32)
     return pl.pallas_call(
         scatter_kernel,
-        out_shape=jax.ShapeDtypeStruct((2, GX, PY, 2, 8, 128), F32),
+        out_shape=(
+            jax.ShapeDtypeStruct((2 * GX * GY, 16, 128), F32),
+            jax.ShapeDtypeStruct((8, 128), jnp.int32),
+            jax.ShapeDtypeStruct((3, 4, 128), F32),
+        ),
         in_specs=[SMEM] * 3 + [HBM] * 5,
-        out_specs=pl.BlockSpec(memory_space=pl.ANY),
+        out_specs=[pl.BlockSpec(memory_space=pl.ANY)] * 3,
         scratch_shapes=[
             pltpu.VMEM((3, NB, 128), F32),
             pltpu.VMEM((3, NB, 128), F32),
@@ -478,40 +561,53 @@
             pltpu.VMEM(((NB + 1) * ROWS, 128), F32),
             pltpu.VMEM((33, 17, 8, 128), F32),
             chunks, chunks, chunks,
-            pltpu.VMEM((2, 8, 128), F32),
+            pltpu.VMEM((3, 4, 128), F32),
             pltpu.VMEM((GX * PY, 2, 8, 128), F32),
-            dma((5,)), dma, dma((GX,)), dma((GX,)), dma, dma, dma((2,)), dma((GX,)), dma((GX,)),
-            dma((GX,)),
+            pltpu.VMEM((2, GX, PY, 3, 4, 128), F32),
+            pltpu.VMEM((33, 17, 8, 128), F32),
+            pltpu.VMEM((2 * GX * GY, 16, 128), F32),
+            dma((5,)), dma, dma((GX,)), dma((GX,)), dma, dma, dma, dma((GX,)), dma((GX,)),
+            dma((GX,)), dma((GX,)), dma((2,)),
         ],
         compiler_params=pltpu.CompilerParams(
-            collective_id=0, has_side_effects=True, vmem_limit_bytes=60 * 1024 * 1024
+            collective_id=0, has_side_effects=True, vmem_limit_bytes=LIMIT
         ),
         name="scatter",
     )(dest, counts, params, off, vel, strain, cells, mats)
 
 
-def gather(dest, counts, params, off, strain, cells, mats, node_vel):
+def finish_strain(dest, counts, params, found, strain, mats, slots, mine):
     return pl.pallas_call(
-        gather_kernel,
+        strain_kernel,
         out_shape=(
             jax.ShapeDtypeStruct((3, NB, 128), F32),
             jax.ShapeDtypeStruct((6, NB, 128), F32),
             jax.ShapeDtypeStruct((3, 2, 2, 128), F32),
         ),
-        in_specs=[SMEM] * 3 + [VMEM] * 5,
+        in_specs=[HBM] * 2 + [SMEM] + [HBM] * 5,
         out_specs=(VMEM, VMEM, VMEM),
-        scratch_shapes=[pltpu.VMEM((33, 17, 8, 128), F32), pltpu.VMEM((8 * 24, 128), F32)],
+        scratch_shapes=[
+            pltpu.VMEM((UNROLL * 128, 128), F32),
+            pltpu.SMEM((NB,), jnp.int32),
+            pltpu.SMEM((NB,), jnp.int32),
+            pltpu.SMEM((8, 128), jnp.int32),
+            pltpu.VMEM((6, NB, 128), F32),
+            pltpu.VMEM((NB, 128), jnp.int32),
+            pltpu.VMEM((2 * GX * GY, 16, 128), F32),
+            pltpu.VMEM((3, 4, 128), F32),
+            pltpu.SemaphoreType.DMA((7,)),
+        ],
         compiler_params=pltpu.CompilerParams(vmem_limit_bytes=LIMIT),
-        name="gather",
-    )(dest, counts, params, off, strain, cells, mats, node_vel)
+        name="strain_map",
+    )(dest, counts, params, found, strain, mats, slots, mine)
 
 
 def shards(offsets, velocity, strain, cells, materials, counts, block_dest, material_params):
     off, vel, eps = (jnp.transpose(x, (1, 0, 2)) for x in (offsets, velocity, strain))
     dest = block_dest.reshape(NB)
-    node_vel = scatter(dest, counts, material_params, off, vel, eps, cells, materials)
-    new_vel, new_eps, own = gather(
-        dest, counts, material_params, off, eps, cells, materials, node_vel
+    slots, found, mine = scatter(dest, counts, material_params, off, vel, eps, cells, materials)
+    new_vel, new_eps, own = finish_strain(
+        dest, counts, material_params, found, eps, materials, slots, mine
     )
     return jnp.transpose(new_vel, (1, 0, 2)), jnp.transpose(new_eps, (1, 0, 2)), own
 

time: 50.4 us -> 50.6 us (level)
  Pallas kernels: 48.3 us -> 49.7 us
  local copies, waits for them, and re-layouts: 1.25 us -> 0 us
    pallas_call x2, Pallas kernels: 48.3 us -> 49.7 us  [the longest x1 45.3 us: scatter(): pl.pallas_call(scatter_kernel, out_shape=(jax.ShapeDtypeStruct((2 * GX *...]
    unnamed x16 -> x0, local copies, waits for them, and re-layouts: 1.25 us -> none
where the time goes in v3:
time: 50.6 us; the launch traced here: 50.4 us
  Pallas kernels  49.7 us (98%)
  between operations  0.64 us (1%)
    pallas_call x1, Pallas kernels, scatter(): pl.pallas_call(scatter_kernel, out_shape=(jax.ShapeDtypeStruct((2 * GX *...  45.3 us
    pallas_call x1, Pallas kernels, finish_strain(): pl.pallas_call(strain_kernel, out_shape=(jax.ShapeDtypeStruct((3, NB, 128...  4.42 us

profile of v3, /device:TPU:1, one launch (start us, length us, event | category | flops | bytes accessed | tf_op | source)
XLA Modules:
  0.0 50.4 jit_solution(10546791558898123678)
XLA Ops:
  0.6 45.3 %scatter.1 = (f32[256,16,128]{2,1,0:T(8,128)}, s32[8,128]{1,0:T(8,128)}, f32[3,4,128]{2,1,0:T(4,128)}) custom-call(s32[192]{0:T(256)} %bitcast.10, s32[192]{0:T(256)} %counts_in.1, f32[3,4]{1,0:T(4,128)} %params.3, f32[3,192,128]{2,1,0:T(8,128)} %bitcast.8, f32[3,192,128]{2,1,0:T(8,128)} %bitcast.9, f32[6,192,128]{2,1,0:T(8,128)} %bitcast.6, ...), custom_call_target="tpu_custom_call" | custom-call | tf_op jit(solution)/shard_map/scatter/pallas_call | solution.py:544
  46.0 4.4 %strain_map.1 = (f32[3,192,128]{2,1,0:T(8,128)}, f32[6,192,128]{2,1,0:T(8,128)}, f32[3,2,2,128]{3,2,1,0:T(2,128)}) custom-call(s32[192]{0:T(256)} %bitcast.11, s32[192]{0:T(256)} %counts_in.1, f32[3,4]{1,0:T(4,128)} %params.3, s32[8,128]{1,0:T(8,128)} %get-tuple-element.9.found_in, f32[6,192,128]{2,1,0:T(8,128)} %bitcast.7, s32[192,128]{1,0:T(8,128)} %mats_in.3, ...), custom_call_target="tpu_custom_call" | custom-call | tf_op jit(solution)/shard_map/strain_map/pallas_call | solution.py:580

commit v4 on v3

--- a/solution.py
+++ b/solution.py
@@ -23,13 +23,10 @@
 LIMIT = 60 * 1024 * 1024
 EMPTY = NB
 ROWS = 32
-LAG = 3
-FIRST = 12
+FIRST = 15
+STEPS = 4
 UNROLL = 4
-FAR_FIRST = sorted(
-    ((dz, dx, dy) for dz in range(4) for dx in range(4) for dy in range(4) if dz + dx + dy),
-    key=lambda o: -sum(min(d, 4 - d) for d in o),
-)
+SEND_ORDER = (15, 0, 1, 2, 3, 4, 5, 6, 7, 8, 9, 10, 11, 12, 13, 14)
 
 
 def iota(shape, dim):
@@ -117,15 +114,14 @@
     for i in range(3):
         low, high = d[0][i], d[1][i]
         tiles += [jnp.where(in_y, 0.0, low), jnp.where(in_y, low, high), jnp.where(in_y, high, 0.0)]
-    tiles.append(jnp.zeros((8, 128), F32))
-    full = jnp.concatenate(tiles, axis=0)
-    hi = full.astype(BF16)
-    lo = (full - hi.astype(F32)).astype(BF16)
+    high = [tile.astype(BF16).astype(F32) for tile in tiles]
+    low = [tile - part for tile, part in zip(tiles, high)]
+    parts = jnp.concatenate(high + low, axis=0).astype(BF16)
     z16 = jnp.concatenate([z, z], axis=0).astype(BF16)
     z_all = jnp.concatenate([z16] * 8, axis=0)
     depth = iota((128, 128), 0).astype(F32).astype(BF16)
     hot = jnp.where(depth == z_all, jnp.ones((), BF16), jnp.zeros((), BF16))
-    return hi, lo, hot
+    return parts, hot
 
 
 def contract(left, right):
@@ -239,12 +235,14 @@
 
     def spread(px):
         for gyp in range(GY):
-            left, right = [], []
-            for slot in range(2):
-                hi, lo, hot = node_rows(by_block[blocks[slot, px * GY + gyp]])
-                left += [hi, lo]
-                right += [hot, hot]
-            sums = contract(jnp.concatenate(left, axis=1), jnp.concatenate(right, axis=1))
+            first, second = (
+                node_rows(by_block[blocks[slot, px * GY + gyp]]) for slot in range(2)
+            )
+            sums = contract(
+                jnp.concatenate([first[0], second[0]], axis=1),
+                jnp.concatenate([first[1], second[1]], axis=1),
+            )
+            sums = sums[:72] + sums[72:]
             for i in range(3):
                 for j in range(3):
                     n = i * 3 + j
@@ -294,28 +292,42 @@
         fold(px)
         sib_copy(px).start()
 
-    def chunk(step, carry):
-        px = lax.rem(gx + step, GX)
-        spread(px)
-
-        @pl.when(step == 1)
+    def down(step):
+        return lax.rem(GX - 1 - step, GX)
+
+    def finish_step(step):
+        finish_chunk(lax.rem(gx + down(step), GX))
+
+    def chunks_down(it, carry):
+        for u in range(STEPS):
+            spread(lax.rem(gx + down(it * STEPS + u), GX))
+
+        @pl.when(it == 0)
         def _():
             pl.semaphore_wait(barrier, GX * PY)
 
-        @pl.when(step > 0)
-        def _():
-            finish_chunk(px)
-
-        @pl.when(step > LAG)
-        def _():
-            send_sums(step - LAG)
+        @pl.when(it > 0)
+        def _():
+            finish_step(it * STEPS - 1)
+
+        for u in range(STEPS - 1):
+            finish_step(it * STEPS + u)
+
+        @pl.when(it > 1)
+        def _():
+            send_sums(down(it * STEPS - STEPS - 1))
+
+        @pl.when(it > 0)
+        def _():
+            for u in range(STEPS - 1):
+                send_sums(down(it * STEPS - STEPS + u))
 
         return carry
 
-    lax.fori_loop(0, GX, chunk, 0)
+    lax.fori_loop(0, GX // STEPS, chunks_down, 0)
     finish_chunk(gx)
-    for step in range(GX - LAG, GX):
-        send_sums(step)
+    for step in range(GX - STEPS - 1, GX - 1):
+        send_sums(down(step))
     add_sib(0)
     for dy in range(1, PY):
         sum_copy(0, dy).start()
@@ -336,16 +348,17 @@
             for c in range(3):
                 mine[c, x * 2 + yn : x * 2 + yn + 1, :] = value[yn * 4 + c : yn * 4 + c + 1]
 
-    z, x4 = gx // 4, lax.rem(gx, 4)
-    turn = 1 - 2 * core
-    for dz, dx, dy in FAR_FIRST:
-        pz = lax.rem(z + turn * dz + 4, 4)
-        px = lax.rem(x4 + turn * dx + 4, 4)
-        py = lax.rem(y + turn * dy + 4, 4)
-        pltpu.make_async_remote_copy(
+    def vel_copy(step, dy):
+        device = peer(GX - step, dy)[2]
+        return pltpu.make_async_remote_copy(
             src_ref=mine, dst_ref=node_vel.at[core, gx, y], send_sem=vel_send,
-            recv_sem=vel_recv.at[gx], device_id=(pz * 4 + px, py * 2 + core), device_id_type=MESH,
-        ).start()
+            recv_sem=vel_recv.at[gx], device_id=device, device_id_type=MESH,
+        )
+
+    for step in SEND_ORDER:
+        for dy in range(PY):
+            if step or dy:
+                vel_copy(step, dy).start()
     node_vel[core, gx, y] = mine[...]
     mine_copy = pltpu.make_async_copy(mine, mine_out, small_sem.at[1])
     mine_copy.start()
@@ -362,12 +375,12 @@
     def pass_on(step):
         px = order(step)
 
-        @pl.when(step == GX - FIRST)
+        @pl.when(px == gx)
         def _():
             few = node_vel.at[core, px, pl.ds(0, PY - 1)]
             pltpu.make_async_copy(few, few, vel_recv.at[px]).wait()
 
-        @pl.when(step != GX - FIRST)
+        @pl.when(px != gx)
         def _():
             here = node_vel.at[core, px]
             pltpu.make_async_copy(here, here, vel_recv.at[px]).wait()
@@ -435,24 +448,32 @@
         at = pl.ds(px * (2 * GY), 2 * GY)
         return pltpu.make_async_copy(slots.at[at], slots_out.at[at], out_sem.at[px])
 
-    pass_on(0)
-    pass_on(1)
-    build(0)
-
-    def gather_chunk(step, carry):
-        @pl.when(step < GX - 2)
-        def _():
-            pass_on(step + 2)
-
-        @pl.when(step < GX - 1)
-        def _():
-            build(step + 1)
-
+    def pick_step(step):
         pick(order(step))
         slots_copy(order(step)).start()
+
+    for step in range(STEPS):
+        pass_on(step)
+
+    def gather_chunks(it, carry):
+        @pl.when(it < GX // STEPS - 1)
+        def _():
+            for u in range(STEPS):
+                pass_on(it * STEPS + STEPS + u)
+
+        for u in range(STEPS):
+            build(it * STEPS + u)
+
+        @pl.when(it > 0)
+        def _():
+            pick_step(it * STEPS - 1)
+
+        for u in range(STEPS - 1):
+            pick_step(it * STEPS + u)
         return carry
 
-    lax.fori_loop(0, GX, gather_chunk, 0)
+    lax.fori_loop(0, GX // STEPS, gather_chunks, 0)
+    pick_step(GX - 1)
 
     def finish(px, carry):
         sib_copy(px).wait_send()

time: 50.6 us -> 42.9 us (0.85)
  Pallas kernels: 49.7 us -> 42.1 us
    pallas_call x1, Pallas kernels: 45.3 us -> 37.6 us  [scatter(): pl.pallas_call(scatter_kernel, out_shape=(jax.ShapeDtypeStruct((2 * GX *...]
where the time goes in v4:
time: 42.9 us; the launch traced here: 42.7 us
  Pallas kernels  42.1 us (98%)
  between operations  0.64 us (1%)
    pallas_call x1, Pallas kernels, scatter(): pl.pallas_call(scatter_kernel, out_shape=(jax.ShapeDtypeStruct((2 * GX *...  37.6 us
    pallas_call x1, Pallas kernels, finish_strain(): pl.pallas_call(strain_kernel, out_shape=(jax.ShapeDtypeStruct((3, NB, 128...  4.43 us

profile of v4, /device:TPU:1, one launch (start us, length us, event | category | flops | bytes accessed | tf_op | source)
XLA Modules:
  0.0 42.7 jit_solution(5919412444660790745)
XLA Ops:
  0.6 37.6 %scatter.1 = (f32[256,16,128]{2,1,0:T(8,128)}, s32[8,128]{1,0:T(8,128)}, f32[3,4,128]{2,1,0:T(4,128)}) custom-call(s32[192]{0:T(256)} %bitcast.10, s32[192]{0:T(256)} %counts_in.1, f32[3,4]{1,0:T(4,128)} %params.3, f32[3,192,128]{2,1,0:T(8,128)} %bitcast.8, f32[3,192,128]{2,1,0:T(8,128)} %bitcast.9, f32[6,192,128]{2,1,0:T(8,128)} %bitcast.6, ...), custom_call_target="tpu_custom_call" | custom-call | tf_op jit(solution)/shard_map/scatter/pallas_call | solution.py:565
  38.3 4.4 %strain_map.1 = (f32[3,192,128]{2,1,0:T(8,128)}, f32[6,192,128]{2,1,0:T(8,128)}, f32[3,2,2,128]{3,2,1,0:T(2,128)}) custom-call(s32[192]{0:T(256)} %bitcast.11, s32[192]{0:T(256)} %counts_in.1, f32[3,4]{1,0:T(4,128)} %params.3, s32[8,128]{1,0:T(8,128)} %get-tuple-element.9.found_in, f32[6,192,128]{2,1,0:T(8,128)} %bitcast.7, s32[192,128]{1,0:T(8,128)} %mats_in.3, ...), custom_call_target="tpu_custom_call" | custom-call | tf_op jit(solution)/shard_map/strain_map/pallas_call | solution.py:601

commit v5 on v4

--- a/solution.py
+++ b/solution.py
@@ -160,11 +160,12 @@
 
 
 def scatter_kernel(
-    dest, counts, params, off_in, vel_in, strain_in, cells_in, mats_in, slots_out, found_out, mine_out,
+    dest_in, counts_in, params, off_in, vel_in, strain_in, cells_in, mats_in,
+    new_vel, new_strain, own,
+    dest, counts, lines,
     off, vel, strain, cells, mats, found, blocks, rows, acc, part, for_sib, from_sib, mine, landed,
     node_vel, table, slots,
     in_sem, found_sem, sib_send, sib_recv, sum_send, sum_recv, vel_send, vel_recv, fwd_send, fwd_recv,
-    out_sem, small_sem,
 ):
     gx = lax.axis_index("gx")
     gy = lax.axis_index("gy")
@@ -182,6 +183,8 @@
         pltpu.make_async_copy(src, dst, in_sem.at[k])
         for k, (src, dst) in enumerate(
             (
+                (dest_in, dest),
+                (counts_in, counts),
                 (off_in, off),
                 (vel_in, vel),
                 (strain_in, strain),
@@ -205,11 +208,10 @@
     for dy in range(1, PY):
         pl.semaphore_signal(barrier, inc=1, device_id=peer(0, dy)[2], device_id_type=MESH)
 
+    loads[0].wait()
     found[...] = find_blocks(dest)
     to_scalars = pltpu.make_async_copy(found, blocks, found_sem)
     to_scalars.start()
-    found_copy = pltpu.make_async_copy(found, found_out, small_sem.at[0])
-    found_copy.start()
 
     rows[NB * ROWS : (NB + 1) * ROWS, :] = jnp.zeros((ROWS, 128), F32)
     by_block = rows.reshape(NB + 1, ROWS, 128)
@@ -223,14 +225,15 @@
         table[x, 16] = jnp.zeros((8, 128), F32)
     for yn in range(16):
         table[32, yn] = jnp.zeros((8, 128), F32)
-    for load in loads:
+    for load in loads[1:]:
         load.wait()
 
-    def prepare(group, carry):
-        source_rows(counts, params, off, vel, strain, cells, mats, rows, group)
+    def prepare(pair, carry):
+        for u in range(2):
+            source_rows(counts, params, off, vel, strain, cells, mats, rows, pair * 2 + u)
         return carry
 
-    lax.fori_loop(0, NB // 8, prepare, 0)
+    lax.fori_loop(0, NB // 16, prepare, 0)
     to_scalars.wait()
 
     def spread(px):
@@ -346,7 +349,9 @@
         value = update(total[x])
         for yn in range(2):
             for c in range(3):
-                mine[c, x * 2 + yn : x * 2 + yn + 1, :] = value[yn * 4 + c : yn * 4 + c + 1]
+                line = value[yn * 4 + c : yn * 4 + c + 1]
+                mine[c, x * 2 + yn : x * 2 + yn + 1, :] = line
+                own[c, x, yn : yn + 1, :] = line
 
     def vel_copy(step, dy):
         device = peer(GX - step, dy)[2]
@@ -360,8 +365,6 @@
             if step or dy:
                 vel_copy(step, dy).start()
     node_vel[core, gx, y] = mine[...]
-    mine_copy = pltpu.make_async_copy(mine, mine_out, small_sem.at[1])
-    mine_copy.start()
 
     def forward(px):
         return pltpu.make_async_remote_copy(
@@ -444,13 +447,8 @@
                 slots[patch * 2 + slot, 0:8, :] = jnp.where(low_half, value, dz)
                 slots[patch * 2 + slot, 8:16, :] = jnp.where(low_half, dx, dy)
 
-    def slots_copy(px):
-        at = pl.ds(px * (2 * GY), 2 * GY)
-        return pltpu.make_async_copy(slots.at[at], slots_out.at[at], out_sem.at[px])
-
     def pick_step(step):
         pick(order(step))
-        slots_copy(order(step)).start()
 
     for step in range(STEPS):
         pass_on(step)
@@ -474,58 +472,13 @@
 
     lax.fori_loop(0, GX // STEPS, gather_chunks, 0)
     pick_step(GX - 1)
-
-    def finish(px, carry):
-        sib_copy(px).wait_send()
-        forward(px).wait_send()
-        slots_copy(px).wait()
-        return carry
-
-    lax.fori_loop(0, GX, finish, 0)
-    pltpu.make_async_copy(many, many, sum_send).wait()
-    own_vel = node_vel.at[core, pl.ds(0, GX - 1)]
-    pltpu.make_async_copy(own_vel, own_vel, vel_send).wait()
-    own_few = node_vel.at[core, 0, pl.ds(0, PY - 1)]
-    pltpu.make_async_copy(own_few, own_few, vel_send).wait()
-    found_copy.wait()
-    mine_copy.wait()
-
-
-def strain_kernel(
-    dest_in, counts_in, params, found_in, strain_in, mats_in, slots_in, mine_in,
-    out_vel, out_strain, out_node,
-    lines, dest, counts, found, strain, mats, slots, mine, in_sem,
-):
-    loads = [
-        pltpu.make_async_copy(src, dst, in_sem.at[k])
-        for k, (src, dst) in enumerate(
-            (
-                (slots_in, slots),
-                (strain_in, strain),
-                (mats_in, mats),
-                (dest_in, dest),
-                (counts_in, counts),
-                (found_in, found),
-                (mine_in, mine),
-            )
-        )
-    ]
-    for load in loads:
-        load.start()
-    for load in loads:
-        load.wait()
-
-    for x in range(2):
-        for yn in range(2):
-            for c in range(3):
-                out_node[c, x, yn : yn + 1, :] = mine[c, x * 2 + yn : x * 2 + yn + 1, :]
 
     def one_group(group, lane):
         at = pl.ds(pl.multiple_of(group * 8, 8), 8)
         for s in range(8):
             block = group * 8 + s
             d = dest[block]
-            slot = d * 2 + jnp.where(found[0, d] == block, 0, 1)
+            slot = d * 2 + jnp.where(blocks[0, d] == block, 0, 1)
             lines[lane * 128 + s * 16 : lane * 128 + s * 16 + 16, :] = slots[slot]
 
         def row(r):
@@ -547,9 +500,9 @@
         )
         factor = limit / jnp.maximum(size, limit)
         for k in range(3):
-            out_vel[k, at, :] = jnp.where(live, speed[k], 0.0)
-            out_strain[k, at, :] = jnp.where(live, mean + factor * dev[k], 0.0)
-            out_strain[3 + k, at, :] = jnp.where(live, factor * dev[3 + k], 0.0)
+            new_vel[k, at, :] = jnp.where(live, speed[k], 0.0)
+            new_strain[k, at, :] = jnp.where(live, mean + factor * dev[k], 0.0)
+            new_strain[3 + k, at, :] = jnp.where(live, factor * dev[3 + k], 0.0)
 
     def groups(step, carry):
         for lane in range(UNROLL):
@@ -557,6 +510,18 @@
         return carry
 
     lax.fori_loop(0, NB // 8 // UNROLL, groups, 0)
+
+    def finish(px, carry):
+        sib_copy(px).wait_send()
+        forward(px).wait_send()
+        return carry
+
+    lax.fori_loop(0, GX, finish, 0)
+    pltpu.make_async_copy(many, many, sum_send).wait()
+    own_vel = node_vel.at[core, pl.ds(0, GX - 1)]
+    pltpu.make_async_copy(own_vel, own_vel, vel_send).wait()
+    own_few = node_vel.at[core, 0, pl.ds(0, PY - 1)]
+    pltpu.make_async_copy(own_few, own_few, vel_send).wait()
 
 
 def scatter(dest, counts, params, off, vel, strain, cells, mats):
@@ -565,13 +530,16 @@
     return pl.pallas_call(
         scatter_kernel,
         out_shape=(
-            jax.ShapeDtypeStruct((2 * GX * GY, 16, 128), F32),
-            jax.ShapeDtypeStruct((8, 128), jnp.int32),
-            jax.ShapeDtypeStruct((3, 4, 128), F32),
+            pltpu.VMEM((3, NB, 128), F32),
+            pltpu.VMEM((6, NB, 128), F32),
+            pltpu.VMEM((3, 2, 2, 128), F32),
         ),
-        in_specs=[SMEM] * 3 + [HBM] * 5,
-        out_specs=[pl.BlockSpec(memory_space=pl.ANY)] * 3,
+        in_specs=[HBM] * 2 + [SMEM] + [HBM] * 5,
+        out_specs=[VMEM] * 3,
         scratch_shapes=[
+            pltpu.SMEM((NB,), jnp.int32),
+            pltpu.SMEM((NB,), jnp.int32),
+            pltpu.VMEM((UNROLL * 128, 128), F32),
             pltpu.VMEM((3, NB, 128), F32),
             pltpu.VMEM((3, NB, 128), F32),
             pltpu.VMEM((6, NB, 128), F32),
@@ -587,8 +555,8 @@
             pltpu.VMEM((2, GX, PY, 3, 4, 128), F32),
             pltpu.VMEM((33, 17, 8, 128), F32),
             pltpu.VMEM((2 * GX * GY, 16, 128), F32),
-            dma((5,)), dma, dma((GX,)), dma((GX,)), dma, dma, dma, dma((GX,)), dma((GX,)),
-            dma((GX,)), dma((GX,)), dma((2,)),
+            dma((7,)), dma, dma((GX,)), dma((GX,)), dma, dma, dma, dma((GX,)), dma((GX,)),
+            dma((GX,)),
         ],
         compiler_params=pltpu.CompilerParams(
             collective_id=0, has_side_effects=True, vmem_limit_bytes=LIMIT
@@ -597,39 +565,34 @@
     )(dest, counts, params, off, vel, strain, cells, mats)
 
 
-def finish_strain(dest, counts, params, found, strain, mats, slots, mine):
+def copy_kernel(a, b, c, x, y, z, sem):
+    copies = [
+        pltpu.make_async_copy(src, dst, sem.at[k])
+        for k, (src, dst) in enumerate(((b, y), (a, x), (c, z)))
+    ]
+    for copy in copies:
+        copy.start()
+    for copy in copies:
+        copy.wait()
+
+
+def hand_out(*arrays):
     return pl.pallas_call(
-        strain_kernel,
-        out_shape=(
-            jax.ShapeDtypeStruct((3, NB, 128), F32),
-            jax.ShapeDtypeStruct((6, NB, 128), F32),
-            jax.ShapeDtypeStruct((3, 2, 2, 128), F32),
-        ),
-        in_specs=[HBM] * 2 + [SMEM] + [HBM] * 5,
-        out_specs=(VMEM, VMEM, VMEM),
-        scratch_shapes=[
-            pltpu.VMEM((UNROLL * 128, 128), F32),
-            pltpu.SMEM((NB,), jnp.int32),
-            pltpu.SMEM((NB,), jnp.int32),
-            pltpu.SMEM((8, 128), jnp.int32),
-            pltpu.VMEM((6, NB, 128), F32),
-            pltpu.VMEM((NB, 128), jnp.int32),
-            pltpu.VMEM((2 * GX * GY, 16, 128), F32),
-            pltpu.VMEM((3, 4, 128), F32),
-            pltpu.SemaphoreType.DMA((7,)),
-        ],
-        compiler_params=pltpu.CompilerParams(vmem_limit_bytes=LIMIT),
-        name="strain_map",
-    )(dest, counts, params, found, strain, mats, slots, mine)
+        copy_kernel,
+        out_shape=tuple(jax.ShapeDtypeStruct(a.shape, a.dtype) for a in arrays),
+        in_specs=[VMEM] * 3,
+        out_specs=[HBM] * 3,
+        scratch_shapes=[pltpu.SemaphoreType.DMA((3,))],
+        compiler_params=pltpu.CompilerParams(vmem_limit_bytes=4 * 1024 * 1024),
+        name="hand_out",
+    )(*arrays)
 
 
 def shards(offsets, velocity, strain, cells, materials, counts, block_dest, material_params):
     off, vel, eps = (jnp.transpose(x, (1, 0, 2)) for x in (offsets, velocity, strain))
     dest = block_dest.reshape(NB)
-    slots, found, mine = scatter(dest, counts, material_params, off, vel, eps, cells, materials)
-    new_vel, new_eps, own = finish_strain(
-        dest, counts, material_params, found, eps, materials, slots, mine
-    )
+    new_vel, new_eps, own = scatter(dest, counts, material_params, off, vel, eps, cells, materials)
+    new_vel, new_eps, own = hand_out(new_vel, new_eps, own)
     return jnp.transpose(new_vel, (1, 0, 2)), jnp.transpose(new_eps, (1, 0, 2)), own
 
 

time: 42.9 us -> 39.6 us (0.923)
  Pallas kernels: 42.1 us -> 38.9 us
    pallas_call x2, Pallas kernels: 42.1 us -> 38.9 us  [the longest x1 37.9 us: scatter(): pl.pallas_call(scatter_kernel, out_shape=(pltpu.VMEM((3, NB, 128), F32),...]
where the time goes in v5:
time: 39.6 us; the launch traced here: 39.5 us
  Pallas kernels  38.9 us (98%)
  between operations  0.64 us (2%)
    pallas_call x1, Pallas kernels, scatter(): pl.pallas_call(scatter_kernel, out_shape=(pltpu.VMEM((3, NB, 128), F32),...  37.9 us
    pallas_call x1, Pallas kernels, hand_out(): pl.pallas_call(copy_kernel, out_shape=tuple((jax.ShapeDtypeStruct(a.shape...  0.94 us

profile of v5, /device:TPU:1, one launch (start us, length us, event | category | flops | bytes accessed | tf_op | source)
XLA Modules:
  0.0 39.5 jit_solution(1801141078911004227)
XLA Ops:
  0.6 37.9 %scatter.1 = (f32[3,192,128]{2,1,0:T(8,128)S(1)}, f32[6,192,128]{2,1,0:T(8,128)S(1)}, f32[3,2,2,128]{3,2,1,0:T(2,128)S(1)}) custom-call(s32[192]{0:T(256)} %bitcast.9, s32[192]{0:T(256)} %counts_in.1, f32[3,4]{1,0:T(4,128)} %params.1, f32[3,192,128]{2,1,0:T(8,128)} %bitcast.7, f32[3,192,128]{2,1,0:T(8,128)} %bitcast.8, f32[6,192,128]{2,1,0:T(8,128)} %bitcast.6, ...), custom_call_target="tpu_custom_call" | custom-call | tf_op jit(solution)/shard_map/scatter/pallas_call | solution.py:530
  38.6 0.9 %hand_out.1 = (f32[3,192,128]{2,1,0:T(8,128)}, f32[6,192,128]{2,1,0:T(8,128)}, f32[3,2,2,128]{3,2,1,0:T(2,128)}) custom-call(f32[3,192,128]{2,1,0:T(8,128)S(1)} %get-tuple-element.9.a, f32[6,192,128]{2,1,0:T(8,128)S(1)} %get-tuple-element.10.b, f32[3,2,2,128]{3,2,1,0:T(2,128)S(1)} %get-tuple-element.11.c), custom_call_target="tpu_custom_call" | custom-call | tf_op jit(solution)/shard_map/hand_out/pallas_call | solution.py:580

commit v6 on v5

--- a/solution.py
+++ b/solution.py
@@ -22,10 +22,17 @@
 HBM = pl.BlockSpec(memory_space=pltpu.HBM)
 LIMIT = 60 * 1024 * 1024
 EMPTY = NB
-ROWS = 32
+ROWS = 40
+LINES = 24
+PAIR = 4
+HOLD = 1
 FIRST = 15
 STEPS = 4
 UNROLL = 4
+FAR_FIRST = sorted(
+    ((dz, dx, dy) for dz in range(4) for dx in range(4) for dy in range(4) if dz + dx + dy),
+    key=lambda o: -sum(min(d, 4 - d) for d in o),
+)
 SEND_ORDER = (15, 0, 1, 2, 3, 4, 5, 6, 7, 8, 9, 10, 11, 12, 13, 14)
 
 
@@ -160,9 +167,9 @@
 
 
 def scatter_kernel(
-    dest_in, counts_in, params, off_in, vel_in, strain_in, cells_in, mats_in,
+    dest_in, counts_in, params_in, off_in, vel_in, strain_in, cells_in, mats_in,
     new_vel, new_strain, own,
-    dest, counts, lines,
+    dest, counts, params, lines,
     off, vel, strain, cells, mats, found, blocks, rows, acc, part, for_sib, from_sib, mine, landed,
     node_vel, table, slots,
     in_sem, found_sem, sib_send, sib_recv, sum_send, sum_recv, vel_send, vel_recv, fwd_send, fwd_recv,
@@ -185,6 +192,7 @@
             (
                 (dest_in, dest),
                 (counts_in, counts),
+                (params_in, params),
                 (off_in, off),
                 (vel_in, vel),
                 (strain_in, strain),
@@ -197,16 +205,10 @@
         load.start()
 
     barrier = pltpu.get_barrier_semaphore()
+    for dz, dx, dy in FAR_FIRST:
+        near = (lax.rem(gx // 4 + dz, 4) * 4 + lax.rem(gx + dx, 4), lax.rem(y + dy, PY) * 2 + core)
+        pl.semaphore_signal(barrier, inc=1, device_id=near, device_id_type=MESH)
     pl.semaphore_signal(barrier, inc=1, device_id=sibling, device_id_type=MESH)
-
-    def greet(step, carry):
-        for dy in range(PY):
-            pl.semaphore_signal(barrier, inc=1, device_id=peer(step, dy)[2], device_id_type=MESH)
-        return carry
-
-    lax.fori_loop(1, GX, greet, 0)
-    for dy in range(1, PY):
-        pl.semaphore_signal(barrier, inc=1, device_id=peer(0, dy)[2], device_id_type=MESH)
 
     loads[0].wait()
     found[...] = find_blocks(dest)
@@ -291,46 +293,50 @@
         for dy in range(PY):
             sum_copy(step, dy).start()
 
-    def finish_chunk(px):
-        fold(px)
-        sib_copy(px).start()
-
     def down(step):
         return lax.rem(GX - 1 - step, GX)
 
-    def finish_step(step):
-        finish_chunk(lax.rem(gx + down(step), GX))
+    def at(step):
+        return lax.rem(gx + down(step), GX)
+
+    def send_part(step, carry):
+        sib_copy(at(step)).start()
+        return carry
+
+    def send_sum(step, carry):
+        send_sums(down(step))
+        return carry
+
+    def to_sibling(it):
+        return jnp.where(it < HOLD, 0, (it + 1) * STEPS - 1)
+
+    def to_owners(it):
+        return jnp.where(it <= HOLD, 0, it * STEPS - 1)
 
     def chunks_down(it, carry):
         for u in range(STEPS):
-            spread(lax.rem(gx + down(it * STEPS + u), GX))
-
-        @pl.when(it == 0)
+            spread(at(it * STEPS + u))
+
+        @pl.when(it > 0)
+        def _():
+            fold(at(it * STEPS - 1))
+
+        for u in range(STEPS - 1):
+            fold(at(it * STEPS + u))
+
+        @pl.when(it == HOLD)
         def _():
             pl.semaphore_wait(barrier, GX * PY)
 
-        @pl.when(it > 0)
-        def _():
-            finish_step(it * STEPS - 1)
-
-        for u in range(STEPS - 1):
-            finish_step(it * STEPS + u)
-
-        @pl.when(it > 1)
-        def _():
-            send_sums(down(it * STEPS - STEPS - 1))
-
-        @pl.when(it > 0)
-        def _():
-            for u in range(STEPS - 1):
-                send_sums(down(it * STEPS - STEPS + u))
-
+        lax.fori_loop(to_sibling(it - 1), to_sibling(it), send_part, 0)
+        lax.fori_loop(to_owners(it - 1), to_owners(it), send_sum, 0)
         return carry
 
     lax.fori_loop(0, GX // STEPS, chunks_down, 0)
-    finish_chunk(gx)
-    for step in range(GX - STEPS - 1, GX - 1):
-        send_sums(down(step))
+    fold(gx)
+    sib_copy(gx).start()
+    first = max(0, GX - STEPS - 1) if HOLD < GX // STEPS - 1 else 0
+    lax.fori_loop(first, GX - 1, send_sum, 0)
     add_sib(0)
     for dy in range(1, PY):
         sum_copy(0, dy).start()
@@ -450,27 +456,27 @@
     def pick_step(step):
         pick(order(step))
 
-    for step in range(STEPS):
+    for step in range(PAIR):
         pass_on(step)
 
     def gather_chunks(it, carry):
-        @pl.when(it < GX // STEPS - 1)
+        @pl.when(it < GX // PAIR - 1)
         def _():
-            for u in range(STEPS):
-                pass_on(it * STEPS + STEPS + u)
-
-        for u in range(STEPS):
-            build(it * STEPS + u)
+            for u in range(PAIR):
+                pass_on((it + 1) * PAIR + u)
+
+        for u in range(PAIR):
+            build(it * PAIR + u)
 
         @pl.when(it > 0)
         def _():
-            pick_step(it * STEPS - 1)
-
-        for u in range(STEPS - 1):
-            pick_step(it * STEPS + u)
-        return carry
-
-    lax.fori_loop(0, GX // STEPS, gather_chunks, 0)
+            pick_step(it * PAIR - 1)
+
+        for u in range(PAIR - 1):
+            pick_step(it * PAIR + u)
+        return carry
+
+    lax.fori_loop(0, GX // PAIR, gather_chunks, 0)
     pick_step(GX - 1)
 
     def one_group(group, lane):
@@ -479,10 +485,11 @@
             block = group * 8 + s
             d = dest[block]
             slot = d * 2 + jnp.where(blocks[0, d] == block, 0, 1)
-            lines[lane * 128 + s * 16 : lane * 128 + s * 16 + 16, :] = slots[slot]
+            first = (lane * 8 + s) * LINES
+            lines[first : first + 16, :] = slots[slot]
 
         def row(r):
-            return lines[pl.ds(lane * 128 + r, 8, stride=16), :]
+            return lines[pl.ds(lane * 8 * LINES + r, 8, stride=LINES), :]
 
         speed = [row(c) for c in range(3)]
         grads = [(row(8 + c), row(12 + c), -row(4 + c)) for c in range(3)]
@@ -534,12 +541,13 @@
             pltpu.VMEM((6, NB, 128), F32),
             pltpu.VMEM((3, 2, 2, 128), F32),
         ),
-        in_specs=[HBM] * 2 + [SMEM] + [HBM] * 5,
+        in_specs=[HBM] * 8,
         out_specs=[VMEM] * 3,
         scratch_shapes=[
             pltpu.SMEM((NB,), jnp.int32),
             pltpu.SMEM((NB,), jnp.int32),
-            pltpu.VMEM((UNROLL * 128, 128), F32),
+            pltpu.SMEM((3, 4), F32),
+            pltpu.VMEM((UNROLL * 8 * LINES, 128), F32),
             pltpu.VMEM((3, NB, 128), F32),
             pltpu.VMEM((3, NB, 128), F32),
             pltpu.VMEM((6, NB, 128), F32),
@@ -555,7 +563,7 @@
             pltpu.VMEM((2, GX, PY, 3, 4, 128), F32),
             pltpu.VMEM((33, 17, 8, 128), F32),
             pltpu.VMEM((2 * GX * GY, 16, 128), F32),
-            dma((7,)), dma, dma((GX,)), dma((GX,)), dma, dma, dma, dma((GX,)), dma((GX,)),
+            dma((8,)), dma, dma((GX,)), dma((GX,)), dma, dma, dma, dma((GX,)), dma((GX,)),
             dma((GX,)),
         ],
         compiler_params=pltpu.CompilerParams(

time: 39.6 us -> 37 us (0.934)
  Pallas kernels: 38.9 us -> 36.2 us
    pallas_call x1, Pallas kernels: 37.9 us -> 35.3 us  [scatter(): pl.pallas_call(scatter_kernel, out_shape=(pltpu.VMEM((3, NB, 128), F32),...]
where the time goes in v6:
time: 37 us; the launch traced here: 36.9 us
  Pallas kernels  36.2 us (98%)
  between operations  0.64 us (2%)
    pallas_call x1, Pallas kernels, scatter(): pl.pallas_call(scatter_kernel, out_shape=(pltpu.VMEM((3, NB, 128), F32),...  35.3 us
    pallas_call x1, Pallas kernels, hand_out(): pl.pallas_call(copy_kernel, out_shape=tuple((jax.ShapeDtypeStruct(a.shape...  0.94 us

profile of v6, /device:TPU:1, one launch (start us, length us, event | category | flops | bytes accessed | tf_op | source)
XLA Modules:
  0.0 36.9 jit_solution(7576215552178829411)
XLA Ops:
  0.6 35.3 %scatter.1 = (f32[3,192,128]{2,1,0:T(8,128)S(1)}, f32[6,192,128]{2,1,0:T(8,128)S(1)}, f32[3,2,2,128]{3,2,1,0:T(2,128)S(1)}) custom-call(s32[192]{0:T(256)} %bitcast.9, s32[192]{0:T(256)} %counts_in.1, f32[3,4]{1,0:T(4,128)} %params_in.1, f32[3,192,128]{2,1,0:T(8,128)} %bitcast.7, f32[3,192,128]{2,1,0:T(8,128)} %bitcast.8, f32[6,192,128]{2,1,0:T(8,128)} %bitcast.6, ...), custom_call_target="tpu_custom_call" | custom-call | tf_op jit(solution)/shard_map/scatter/pallas_call | solution.py:537
  35.9 0.9 %hand_out.1 = (f32[3,192,128]{2,1,0:T(8,128)}, f32[6,192,128]{2,1,0:T(8,128)}, f32[3,2,2,128]{3,2,1,0:T(2,128)}) custom-call(f32[3,192,128]{2,1,0:T(8,128)S(1)} %get-tuple-element.9.a, f32[6,192,128]{2,1,0:T(8,128)S(1)} %get-tuple-element.10.b, f32[3,2,2,128]{3,2,1,0:T(2,128)S(1)} %get-tuple-element.11.c), custom_call_target="tpu_custom_call" | custom-call | tf_op jit(solution)/shard_map/hand_out/pallas_call | solution.py:588

commit v7 on v6

--- a/solution.py
+++ b/solution.py
@@ -24,11 +24,12 @@
 EMPTY = NB
 ROWS = 40
 LINES = 24
-PAIR = 4
+LINE = 17
+BEHIND = 4
 HOLD = 1
 FIRST = 15
 STEPS = 4
-UNROLL = 4
+UNROLL = 3
 FAR_FIRST = sorted(
     ((dz, dx, dy) for dz in range(4) for dx in range(4) for dy in range(4) if dz + dx + dy),
     key=lambda o: -sum(min(d, 4 - d) for d in o),
@@ -94,7 +95,6 @@
     put(26, (cell & (NZ - 1)).astype(F32))
     put(27, cell.astype(F32))
     put(28, (cell & NZ).astype(F32))
-    put(29, fz)
 
 
 def node_rows(source):
@@ -171,7 +171,7 @@
     new_vel, new_strain, own,
     dest, counts, params, lines,
     off, vel, strain, cells, mats, found, blocks, rows, acc, part, for_sib, from_sib, mine, landed,
-    node_vel, table, slots,
+    node_vel, table,
     in_sem, found_sem, sib_send, sib_recv, sum_send, sum_recv, vel_send, vel_recv, fwd_send, fwd_recv,
 ):
     gx = lax.axis_index("gx")
@@ -224,9 +224,9 @@
 
     lax.fori_loop(0, 33, clear, 0)
     for x in range(33):
-        table[x, 16] = jnp.zeros((8, 128), F32)
+        table[x * LINE + 16] = jnp.zeros((8, 128), F32)
     for yn in range(16):
-        table[32, yn] = jnp.zeros((8, 128), F32)
+        table[32 * LINE + yn] = jnp.zeros((8, 128), F32)
     for load in loads[1:]:
         load.wait()
 
@@ -412,87 +412,64 @@
                 )
                 level = jnp.where(sub % 4 == 0, c0, jnp.where(sub % 4 == 1, c1, c2))
                 lifted = jnp.where(below, pltpu.roll(level, NZ - 1, axis=1), 0.0)
-                table[px * 2 + x, yn] = jnp.where(low_half, level, lifted)
-
-    def pick(px):
-        for gyp in range(GY):
-            tiles = [[table[px * 2 + i, gyp * 2 + j] for j in range(3)] for i in range(3)]
-            for slot in range(2):
-                patch = px * GY + gyp
-                misc = by_block[blocks[slot, patch], 24:32, :]
-                fx, fy, cz, in_x, in_y, fz = (
-                    jnp.broadcast_to(misc[k : k + 1], (8, 128)) for k in range(6)
-                )
-                cz = cz.astype(jnp.int32)
-                in_x = in_x >= 2.0 * NZ
-                in_y = in_y > 0.0
-                got = [
-                    [
-                        jnp.take_along_axis(tile, cz, axis=1, mode="promise_in_bounds")
-                        for tile in line
-                    ]
-                    for line in tiles
+                table[(px * 2 + x) * LINE + yn] = jnp.where(low_half, level, lifted)
+
+    def arrive(step, carry):
+        pass_on(step)
+
+        @pl.when(step >= BEHIND)
+        def _():
+            build(step - BEHIND)
+
+        return carry
+
+    lax.fori_loop(0, GX, arrive, 0)
+    lax.fori_loop(GX - BEHIND, GX, lambda step, carry: (build(step), carry)[1], 0)
+
+    def pick(group, lane):
+        at = pl.ds(pl.multiple_of(group * 8, 8), 8)
+        cell8, fx8, fy8 = cells[at, :], off[0, at, :], off[1, at, :]
+        for s in range(8):
+            d = dest[group * 8 + s]
+            corner = d // GY * (2 * LINE) + d % GY * 2
+            cell, fx, fy = (jnp.broadcast_to(v[s : s + 1], (8, 128)) for v in (cell8, fx8, fy8))
+            cz = cell & (NZ - 1)
+            in_x = cell >= 2 * NZ
+            in_y = (cell & NZ) != 0
+            got = [
+                [
+                    jnp.take_along_axis(
+                        table[corner + (i * LINE + j)], cz, axis=1, mode="promise_in_bounds"
+                    )
+                    for j in range(3)
                 ]
-                side = [
-                    [jnp.where(in_y, line[b + 1], line[b]) for b in range(2)] for line in got
-                ]
-                p = [
-                    [jnp.where(in_x, side[a + 1][b], side[a][b]) for b in range(2)]
-                    for a in range(2)
-                ]
-                dy = [p[a][1] - p[a][0] for a in range(2)]
-                ly = [p[a][0] + fy * dy[a] for a in range(2)]
-                dx = ly[1] - ly[0]
-                value = ly[0] + fx * dx
-                dy = dy[0] + fx * (dy[1] - dy[0])
-                part_z = jnp.where(low_half, fz, 1.0 - fz)
-                dz = pltpu.roll(value, 4, axis=0) - value
-                value = value + part_z * dz
-                dx = dx + part_z * (pltpu.roll(dx, 4, axis=0) - dx)
-                dy = dy + part_z * (pltpu.roll(dy, 4, axis=0) - dy)
-                slots[patch * 2 + slot, 0:8, :] = jnp.where(low_half, value, dz)
-                slots[patch * 2 + slot, 8:16, :] = jnp.where(low_half, dx, dy)
-
-    def pick_step(step):
-        pick(order(step))
-
-    for step in range(PAIR):
-        pass_on(step)
-
-    def gather_chunks(it, carry):
-        @pl.when(it < GX // PAIR - 1)
-        def _():
-            for u in range(PAIR):
-                pass_on((it + 1) * PAIR + u)
-
-        for u in range(PAIR):
-            build(it * PAIR + u)
-
-        @pl.when(it > 0)
-        def _():
-            pick_step(it * PAIR - 1)
-
-        for u in range(PAIR - 1):
-            pick_step(it * PAIR + u)
-        return carry
-
-    lax.fori_loop(0, GX // PAIR, gather_chunks, 0)
-    pick_step(GX - 1)
+                for i in range(3)
+            ]
+            side = [[jnp.where(in_y, line[b + 1], line[b]) for b in range(2)] for line in got]
+            p = [[jnp.where(in_x, side[a + 1][b], side[a][b]) for b in range(2)] for a in range(2)]
+            dy = [p[a][1] - p[a][0] for a in range(2)]
+            ly = [p[a][0] + fy * dy[a] for a in range(2)]
+            dx = ly[1] - ly[0]
+            first = (lane * 8 + s) * LINES
+            lines[first : first + 8, :] = ly[0] + fx * dx
+            lines[first + 8 : first + 16, :] = dx
+            lines[first + 16 : first + 24, :] = dy[0] + fx * (dy[1] - dy[0])
 
     def one_group(group, lane):
         at = pl.ds(pl.multiple_of(group * 8, 8), 8)
-        for s in range(8):
-            block = group * 8 + s
-            d = dest[block]
-            slot = d * 2 + jnp.where(blocks[0, d] == block, 0, 1)
-            first = (lane * 8 + s) * LINES
-            lines[first : first + 16, :] = slots[slot]
 
         def row(r):
             return lines[pl.ds(lane * 8 * LINES + r, 8, stride=LINES), :]
 
-        speed = [row(c) for c in range(3)]
-        grads = [(row(8 + c), row(12 + c), -row(4 + c)) for c in range(3)]
+        fz = off[2, at, :]
+        speed = []
+        grads = []
+        for c in range(3):
+            v0 = row(c)
+            dz = row(4 + c) - v0
+            speed.append(v0 + fz * dz)
+            dx, dy = row(8 + c), row(16 + c)
+            grads.append((dx + fz * (row(12 + c) - dx), dy + fz * (row(20 + c) - dy), dz))
         live = live_mask(counts, group)
         limit = by_material(params, 2, mats[at, :])
         e = [strain[k, at, :] for k in range(6)]
@@ -511,12 +488,26 @@
             new_strain[k, at, :] = jnp.where(live, mean + factor * dev[k], 0.0)
             new_strain[3 + k, at, :] = jnp.where(live, factor * dev[3 + k], 0.0)
 
-    def groups(step, carry):
+    def pick_step(step, half):
         for lane in range(UNROLL):
-            one_group(step * UNROLL + lane, lane)
-        return carry
-
-    lax.fori_loop(0, NB // 8 // UNROLL, groups, 0)
+            pick(step * UNROLL + lane, half * UNROLL + lane)
+
+    def map_step(step, half):
+        for lane in range(UNROLL):
+            one_group(step * UNROLL + lane, half * UNROLL + lane)
+
+    def groups(pair, carry):
+        for half in range(2):
+            pick_step(pair * 2 + half + 1, 1 - half)
+            map_step(pair * 2 + half, half)
+        return carry
+
+    last = NB // 8 // UNROLL - 1
+    pick_step(0, 0)
+    lax.fori_loop(0, last // 2, groups, 0)
+    pick_step(last, 1)
+    map_step(last - 1, 0)
+    map_step(last, 1)
 
     def finish(px, carry):
         sib_copy(px).wait_send()
@@ -547,7 +538,7 @@
             pltpu.SMEM((NB,), jnp.int32),
             pltpu.SMEM((NB,), jnp.int32),
             pltpu.SMEM((3, 4), F32),
-            pltpu.VMEM((UNROLL * 8 * LINES, 128), F32),
+            pltpu.VMEM((2 * UNROLL * 8 * LINES, 128), F32),
             pltpu.VMEM((3, NB, 128), F32),
             pltpu.VMEM((3, NB, 128), F32),
             pltpu.VMEM((6, NB, 128), F32),
@@ -561,8 +552,7 @@
             pltpu.VMEM((3, 4, 128), F32),
             pltpu.VMEM((GX * PY, 2, 8, 128), F32),
             pltpu.VMEM((2, GX, PY, 3, 4, 128), F32),
-            pltpu.VMEM((33, 17, 8, 128), F32),
-            pltpu.VMEM((2 * GX * GY, 16, 128), F32),
+            pltpu.VMEM((33 * LINE, 8, 128), F32),
             dma((8,)), dma, dma((GX,)), dma((GX,)), dma, dma, dma, dma((GX,)), dma((GX,)),
             dma((GX,)),
         ],

time: 37 us -> 36.4 us (0.984)
  Pallas kernels: 36.2 us -> 35.6 us
    pallas_call x1, Pallas kernels: 35.3 us -> 34.6 us  [scatter(): pl.pallas_call(scatter_kernel, out_shape=(pltpu.VMEM((3, NB, 128), F32),...]
where the time goes in v7:
time: 36.4 us; the launch traced here: 36.2 us
  Pallas kernels  35.6 us (98%)
  between operations  0.64 us (2%)
    pallas_call x1, Pallas kernels, scatter(): pl.pallas_call(scatter_kernel, out_shape=(pltpu.VMEM((3, NB, 128), F32),...  34.6 us
    pallas_call x1, Pallas kernels, hand_out(): pl.pallas_call(copy_kernel, out_shape=tuple((jax.ShapeDtypeStruct(a.shape...  0.94 us

profile of v7, /device:TPU:1, one launch (start us, length us, event | category | flops | bytes accessed | tf_op | source)
XLA Modules:
  0.0 36.2 jit_solution(2194009952870717805)
XLA Ops:
  0.6 34.6 %scatter.1 = (f32[3,192,128]{2,1,0:T(8,128)S(1)}, f32[6,192,128]{2,1,0:T(8,128)S(1)}, f32[3,2,2,128]{3,2,1,0:T(2,128)S(1)}) custom-call(s32[192]{0:T(256)} %bitcast.9, s32[192]{0:T(256)} %counts_in.1, f32[3,4]{1,0:T(4,128)} %params_in.1, f32[3,192,128]{2,1,0:T(8,128)} %bitcast.7, f32[3,192,128]{2,1,0:T(8,128)} %bitcast.8, f32[6,192,128]{2,1,0:T(8,128)} %bitcast.6, ...), custom_call_target="tpu_custom_call" | custom-call | tf_op jit(solution)/shard_map/scatter/pallas_call | solution.py:528
  35.3 0.9 %hand_out.1 = (f32[3,192,128]{2,1,0:T(8,128)}, f32[6,192,128]{2,1,0:T(8,128)}, f32[3,2,2,128]{3,2,1,0:T(2,128)}) custom-call(f32[3,192,128]{2,1,0:T(8,128)S(1)} %get-tuple-element.9.a, f32[6,192,128]{2,1,0:T(8,128)S(1)} %get-tuple-element.10.b, f32[3,2,2,128]{3,2,1,0:T(2,128)S(1)} %get-tuple-element.11.c), custom_call_target="tpu_custom_call" | custom-call | tf_op jit(solution)/shard_map/hand_out/pallas_call | solution.py:578

commit v8 on v7

--- a/solution.py
+++ b/solution.py
@@ -25,16 +25,14 @@
 ROWS = 40
 LINES = 24
 LINE = 17
-BEHIND = 4
+BEHIND = 8
 HOLD = 1
-FIRST = 15
 STEPS = 4
 UNROLL = 3
 FAR_FIRST = sorted(
     ((dz, dx, dy) for dz in range(4) for dx in range(4) for dy in range(4) if dz + dx + dy),
     key=lambda o: -sum(min(d, 4 - d) for d in o),
 )
-SEND_ORDER = (15, 0, 1, 2, 3, 4, 5, 6, 7, 8, 9, 10, 11, 12, 13, 14)
 
 
 def iota(shape, dim):
@@ -283,18 +281,23 @@
             recv_sem=sum_recv, device_id=device, device_id_type=MESH,
         )
 
-    def add_sib(step):
+    def send_sums(step):
         px = lax.rem(gx + step, GX)
         sib_copy(px).wait_recv()
         part[px] = part[px] + from_sib[px]
-
-    def send_sums(step):
-        add_sib(step)
-        for dy in range(PY):
+        for dy in (2, 1, 3):
             sum_copy(step, dy).start()
 
+        @pl.when(px != gx)
+        def _():
+            sum_copy(step, 0).start()
+
+        @pl.when(px == gx)
+        def _():
+            landed[chip] = part[gx, y]
+
     def down(step):
-        return lax.rem(GX - 1 - step, GX)
+        return lax.rem(2 * GX + (-1 - lax.rem(gx, 4)) - step, GX)
 
     def at(step):
         return lax.rem(gx + down(step), GX)
@@ -333,14 +336,10 @@
         return carry
 
     lax.fori_loop(0, GX // STEPS, chunks_down, 0)
-    fold(gx)
-    sib_copy(gx).start()
+    fold(at(GX - 1))
+    sib_copy(at(GX - 1)).start()
     first = max(0, GX - STEPS - 1) if HOLD < GX // STEPS - 1 else 0
-    lax.fori_loop(first, GX - 1, send_sum, 0)
-    add_sib(0)
-    for dy in range(1, PY):
-        sum_copy(0, dy).start()
-    landed[chip] = part[gx, y]
+    lax.fori_loop(first, GX, send_sum, 0)
 
     many = landed.at[pl.ds(0, GX * PY - 1)]
     pltpu.make_async_copy(many, many, sum_recv).wait()
@@ -359,17 +358,29 @@
                 mine[c, x * 2 + yn : x * 2 + yn + 1, :] = line
                 own[c, x, yn : yn + 1, :] = line
 
-    def vel_copy(step, dy):
-        device = peer(GX - step, dy)[2]
+    z = gx // 4
+
+    def vel_copy(pz, dx, dy):
+        device = (pz * 4 + lax.rem(gx + dx, 4), lax.rem(y + dy, PY) * 2 + core)
         return pltpu.make_async_remote_copy(
             src_ref=mine, dst_ref=node_vel.at[core, gx, y], send_sem=vel_send,
             recv_sem=vel_recv.at[gx], device_id=device, device_id_type=MESH,
         )
 
-    for step in SEND_ORDER:
-        for dy in range(PY):
-            if step or dy:
-                vel_copy(step, dy).start()
+    def send_row(pz):
+        @pl.when(pz != z)
+        def _():
+            vel_copy(pz, 0, 0).start()
+
+        for dx in (0, 1, 3, 2):
+            for dy in (0, 1, 3, 2):
+                if dx or dy:
+                    vel_copy(pz, dx, dy).start()
+
+    send_row(0)
+    for k in range(3):
+        send_row(1 + lax.rem(z + k + 2, 3))
+
     node_vel[core, gx, y] = mine[...]
 
     def forward(px):
@@ -379,7 +390,9 @@
         )
 
     def order(step):
-        return lax.rem(gx + (FIRST + step), GX)
+        row = step // 4
+        dz = jnp.where(row < 2, row, 5 - row)
+        return lax.rem(gx // 4 + dz, 4) * 4 + lax.rem(gx + step, 4)
 
     def pass_on(step):
         px = order(step)

time: 36.4 us -> 34.7 us (0.953)
  Pallas kernels: 35.6 us -> 33.9 us
    pallas_call x1, Pallas kernels: 34.6 us -> 32.9 us  [scatter(): pl.pallas_call(scatter_kernel, out_shape=(pltpu.VMEM((3, NB, 128), F32),...]
where the time goes in v8:
time: 34.7 us; the launch traced here: 34.5 us
  Pallas kernels  33.9 us (98%)
  between operations  0.64 us (2%)
    pallas_call x1, Pallas kernels, scatter(): pl.pallas_call(scatter_kernel, out_shape=(pltpu.VMEM((3, NB, 128), F32),...  32.9 us
    pallas_call x1, Pallas kernels, hand_out(): pl.pallas_call(copy_kernel, out_shape=tuple((jax.ShapeDtypeStruct(a.shape...  0.94 us

profile of v8, /device:TPU:1, one launch (start us, length us, event | category | flops | bytes accessed | tf_op | source)
XLA Modules:
  0.0 34.5 jit_solution(3758587795551572680)
XLA Ops:
  0.6 32.9 %scatter.1 = (f32[3,192,128]{2,1,0:T(8,128)S(1)}, f32[6,192,128]{2,1,0:T(8,128)S(1)}, f32[3,2,2,128]{3,2,1,0:T(2,128)S(1)}) custom-call(s32[192]{0:T(256)} %bitcast.9, s32[192]{0:T(256)} %counts_in.1, f32[3,4]{1,0:T(4,128)} %params_in.1, f32[3,192,128]{2,1,0:T(8,128)} %bitcast.7, f32[3,192,128]{2,1,0:T(8,128)} %bitcast.8, f32[6,192,128]{2,1,0:T(8,128)} %bitcast.6, ...), custom_call_target="tpu_custom_call" | custom-call | tf_op jit(solution)/shard_map/scatter/pallas_call | solution.py:541
  33.6 0.9 %hand_out.1 = (f32[3,192,128]{2,1,0:T(8,128)}, f32[6,192,128]{2,1,0:T(8,128)}, f32[3,2,2,128]{3,2,1,0:T(2,128)}) custom-call(f32[3,192,128]{2,1,0:T(8,128)S(1)} %get-tuple-element.9.a, f32[6,192,128]{2,1,0:T(8,128)S(1)} %get-tuple-element.10.b, f32[3,2,2,128]{3,2,1,0:T(2,128)S(1)} %get-tuple-element.11.c), custom_call_target="tpu_custom_call" | custom-call | tf_op jit(solution)/shard_map/hand_out/pallas_call | solution.py:591

commit v9 on v8

--- a/solution.py
+++ b/solution.py
@@ -361,21 +361,20 @@
     z = gx // 4
 
     def vel_copy(pz, dx, dy):
-        device = (pz * 4 + lax.rem(gx + dx, 4), lax.rem(y + dy, PY) * 2 + core)
+        device = (pz * 4 + lax.rem(gx + dx, 4), dy * 2 + core)
         return pltpu.make_async_remote_copy(
             src_ref=mine, dst_ref=node_vel.at[core, gx, y], send_sem=vel_send,
             recv_sem=vel_recv.at[gx], device_id=device, device_id_type=MESH,
         )
 
     def send_row(pz):
-        @pl.when(pz != z)
-        def _():
-            vel_copy(pz, 0, 0).start()
-
-        for dx in (0, 1, 3, 2):
-            for dy in (0, 1, 3, 2):
-                if dx or dy:
-                    vel_copy(pz, dx, dy).start()
+        for py in range(PY):
+            @pl.when((pz != z) | (py != y))
+            def _():
+                vel_copy(pz, 0, py).start()
+
+            for dx in (1, 3, 2):
+                vel_copy(pz, dx, py).start()
 
     send_row(0)
     for k in range(3):
@@ -551,7 +550,7 @@
             pltpu.SMEM((NB,), jnp.int32),
             pltpu.SMEM((NB,), jnp.int32),
             pltpu.SMEM((3, 4), F32),
-            pltpu.VMEM((2 * UNROLL * 8 * LINES, 128), F32),
+            pltpu.VMEM(((2 * UNROLL * 8 + 1) * LINES, 128), F32),
             pltpu.VMEM((3, NB, 128), F32),
             pltpu.VMEM((3, NB, 128), F32),
             pltpu.VMEM((6, NB, 128), F32),

time: 34.7 us -> 34.6 us (level)
  no operation moved by 1% of the time
where the time goes in v9:
time: 34.6 us; the launch traced here: 34.5 us
  Pallas kernels  33.9 us (98%)
  between operations  0.64 us (2%)
    pallas_call x1, Pallas kernels, scatter(): pl.pallas_call(scatter_kernel, out_shape=(pltpu.VMEM((3, NB, 128), F32),...  32.9 us
    pallas_call x1, Pallas kernels, hand_out(): pl.pallas_call(copy_kernel, out_shape=tuple((jax.ShapeDtypeStruct(a.shape...  0.94 us

profile of v9, /device:TPU:1, one launch (start us, length us, event | category | flops | bytes accessed | tf_op | source)
XLA Modules:
  0.0 34.5 jit_solution(2352767861012817348)
XLA Ops:
  0.6 32.9 %scatter.1 = (f32[3,192,128]{2,1,0:T(8,128)S(1)}, f32[6,192,128]{2,1,0:T(8,128)S(1)}, f32[3,2,2,128]{3,2,1,0:T(2,128)S(1)}) custom-call(s32[192]{0:T(256)} %bitcast.9, s32[192]{0:T(256)} %counts_in.1, f32[3,4]{1,0:T(4,128)} %params_in.1, f32[3,192,128]{2,1,0:T(8,128)} %bitcast.7, f32[3,192,128]{2,1,0:T(8,128)} %bitcast.8, f32[6,192,128]{2,1,0:T(8,128)} %bitcast.6, ...), custom_call_target="tpu_custom_call" | custom-call | tf_op jit(solution)/shard_map/scatter/pallas_call | solution.py:540
  33.6 0.9 %hand_out.1 = (f32[3,192,128]{2,1,0:T(8,128)}, f32[6,192,128]{2,1,0:T(8,128)}, f32[3,2,2,128]{3,2,1,0:T(2,128)}) custom-call(f32[3,192,128]{2,1,0:T(8,128)S(1)} %get-tuple-element.9.a, f32[6,192,128]{2,1,0:T(8,128)S(1)} %get-tuple-element.10.b, f32[3,2,2,128]{3,2,1,0:T(2,128)S(1)} %get-tuple-element.11.c), custom_call_target="tpu_custom_call" | custom-call | tf_op jit(solution)/shard_map/hand_out/pallas_call | solution.py:590

commit v10 on v9

--- a/solution.py
+++ b/solution.py
@@ -25,7 +25,7 @@
 ROWS = 40
 LINES = 24
 LINE = 17
-BEHIND = 8
+BEHIND = 12
 HOLD = 1
 STEPS = 4
 UNROLL = 3

time: 34.6 us -> 34.5 us (level)
  no operation moved by 1% of the time
where the time goes in v10:
time: 34.5 us; the launch traced here: 34.4 us
  Pallas kernels  33.8 us (98%)
  between operations  0.64 us (2%)
    pallas_call x1, Pallas kernels, scatter(): pl.pallas_call(scatter_kernel, out_shape=(pltpu.VMEM((3, NB, 128), F32),...  32.8 us
    pallas_call x1, Pallas kernels, hand_out(): pl.pallas_call(copy_kernel, out_shape=tuple((jax.ShapeDtypeStruct(a.shape...  0.94 us

profile of v10, /device:TPU:1, one launch (start us, length us, event | category | flops | bytes accessed | tf_op | source)
XLA Modules:
  0.0 34.4 jit_solution(11663601504490163619)
XLA Ops:
  0.6 32.8 %scatter.1 = (f32[3,192,128]{2,1,0:T(8,128)S(1)}, f32[6,192,128]{2,1,0:T(8,128)S(1)}, f32[3,2,2,128]{3,2,1,0:T(2,128)S(1)}) custom-call(s32[192]{0:T(256)} %bitcast.9, s32[192]{0:T(256)} %counts_in.1, f32[3,4]{1,0:T(4,128)} %params_in.1, f32[3,192,128]{2,1,0:T(8,128)} %bitcast.7, f32[3,192,128]{2,1,0:T(8,128)} %bitcast.8, f32[6,192,128]{2,1,0:T(8,128)} %bitcast.6, ...), custom_call_target="tpu_custom_call" | custom-call | tf_op jit(solution)/shard_map/scatter/pallas_call | solution.py:540
  33.5 0.9 %hand_out.1 = (f32[3,192,128]{2,1,0:T(8,128)}, f32[6,192,128]{2,1,0:T(8,128)}, f32[3,2,2,128]{3,2,1,0:T(2,128)}) custom-call(f32[3,192,128]{2,1,0:T(8,128)S(1)} %get-tuple-element.9.a, f32[6,192,128]{2,1,0:T(8,128)S(1)} %get-tuple-element.10.b, f32[3,2,2,128]{3,2,1,0:T(2,128)S(1)} %get-tuple-element.11.c), custom_call_target="tpu_custom_call" | custom-call | tf_op jit(solution)/shard_map/hand_out/pallas_call | solution.py:590
